TPU v7x, 32 devices: a whole 2x2x4 slice. The times are simulated.
32 devices in a mesh: parts: 2 (over y), tile: 4 (over z), src: 2 (over x), focus: 2 (over core).
Axes of the slice: x: 2, y: 2, z: 4, core: 2. Of those that a mesh axis runs over, the one named last changes fastest.
Arguments:
- mask: float32 [768, 1536], P('parts', 'tile'), parts along dimension 0, may hold values from -1 to 1
- target: float32 [768, 1536], P('parts', 'tile'), parts along dimension 0, may hold values from 0 to 1
- pupil: float32 [2, 16, 4, 64, 64], P(None, 'src', 'focus'), may hold values from -6 to 6
- weights: float32 [16], P('src'), may hold values from 0.25 to 4
- counts: int32 [8], P('parts'), parts along dimension 0, may hold values from 1 to 4, as said below
Outputs:
- gradient: float32 [768, 1536], P(('parts', 'src', 'focus'), 'tile'), parts along dimension 0
There are 2 independent parts, one for each index of `parts`. A program takes and returns all parts, laid end to end along the dimension named above; an argument that names none is the same for every part. Nothing has to cross between parts.
Inputs may be any that keep to these rules, and one draw needn't show every extreme that they name: Corners 0 to counts - 1 of a subtile are in use; of the two subtiles t and t + 2 at least one uses a single corner; some subtile uses all 4.
All inputs are finite; a program needn't handle non-finite values.
Results may differ from a plain program's by a relative error of at most 0.0003.
Values sent between devices are 32-bit elements; how exact they have to be, the bound alone decides.
A program may use at most 128 MiB of HBM per device.

v0:
```python
import math

import jax
import jax.numpy as jnp
from jax import lax
from jax.sharding import PartitionSpec as P

AMBIT = 64


resist_slope = 4.0
resist_level = 0.5


def with_halo(block, sides, width):
    for axis, dim in sides:
        count = lax.axis_size(axis)
        forward = [(i, i + 1) for i in range(count - 1)]
        backward = [(target, source) for source, target in forward]
        low = lax.ppermute(
            lax.slice_in_dim(block, block.shape[dim] - width, None, axis=dim), axis, forward
        )
        high = lax.ppermute(lax.slice_in_dim(block, 0, width, axis=dim), axis, backward)
        block = jnp.concatenate([low, block, high], axis=dim)
    return block


def passed_along(value, axis, by):
    peers = lax.axis_size(axis)
    pairs = [(i, i + by) for i in range(peers) if 0 <= i + by < peers]
    return lax.ppermute(value, axis, pairs)


def product(left, right):
    return jnp.dot(left, right, precision=lax.Precision.HIGHEST, preferred_element_type=jnp.float32)


def phase_table(freqs, length, offset, count):
    kvalues = jnp.arange(freqs, dtype=jnp.int32) - freqs // 2
    nvalues = jnp.arange(count, dtype=jnp.int32) + offset
    phase = jnp.mod(kvalues[:, None] * nvalues[None, :], length).astype(jnp.float32) * (
        2.0 * math.pi / length
    )
    return (jnp.cos(phase), jnp.sin(phase))


def add_edges(window_grad, width, tile, from_left, from_right):
    filler = jnp.zeros((window_grad.shape[0], tile - width), jnp.float32)
    middle = window_grad[:, width : width + tile]
    middle = middle + jnp.concatenate([from_left, filler], axis=1)
    return middle + jnp.concatenate([filler, from_right], axis=1)


def per_device(mask, target, pupil, weights, counts):
    tile = mask.shape[0]
    freqs = pupil.shape[-1]
    width = AMBIT
    win = tile + 2 * width
    local_src = weights.shape[0]
    sources = local_src * lax.axis_size("src")
    corner_dev = pupil.shape[2]
    norm_win = 1.0 / math.sqrt(win)
    norm_back = math.sqrt(2.0 / freqs)
    cos_col, sin_col = phase_table(freqs, win, 0, win)
    col_re = cos_col * norm_win
    col_im = -sin_col * norm_win
    cos_row, sin_row = phase_table(freqs, win, width, tile)
    row_re = cos_row * norm_win
    row_im = -sin_row * norm_win
    back_re = cos_row.T * norm_back
    back_im = sin_row.T * norm_back
    back_re_t = cos_row * norm_back
    back_im_t = sin_row * norm_back
    src_scale = weights / sources
    extended = with_halo(mask, (("tile", 1),), width)
    x_re = product(extended, col_re.T)
    x_im = product(extended, col_im.T)
    spec_re = product(row_re, x_re) - product(row_im, x_im)
    spec_im = product(row_re, x_im) + product(row_im, x_re)
    tile_index = lax.axis_index("tile")
    focus_index = lax.axis_index("focus")
    own_load = jnp.clip(counts[tile_index] - focus_index * corner_dev, 0, corner_dev)
    pup_re = pupil[0]
    pup_im = pupil[1]
    zero_int = jnp.zeros((), jnp.int32)
    source_count = jnp.asarray(local_src, jnp.int32)

    def fields(g_re, g_im):
        h_re = product(g_re, back_re_t) - product(g_im, back_im_t)
        h_im = product(g_re, back_im_t) + product(g_im, back_re_t)
        e_re = product(back_re, h_re) - product(back_im, h_im)
        e_im = product(back_re, h_im) + product(back_im, h_re)
        return (e_re, e_im)

    keeps = []
    for corner in range(corner_dev):
        keeps.append(
            jnp.where(
                corner < own_load - 1,
                source_count,
                jnp.where(corner == own_load - 1, source_count, zero_int),
            )
        )
    store_shape = (corner_dev * local_src, tile, tile)
    stores = (jnp.zeros(store_shape, jnp.float32), jnp.zeros(store_shape, jnp.float32))
    offsets = []
    offset = zero_int
    partials = []
    for corner in range(corner_dev):
        offsets.append(offset)
        forward_corner_re = pup_re[:, corner]
        forward_corner_im = pup_im[:, corner]

        def forward_add_source(source, carry):
            total, store_re, store_im = carry
            p_re = lax.dynamic_index_in_dim(forward_corner_re, source, 0, keepdims=False)
            p_im = lax.dynamic_index_in_dim(forward_corner_im, source, 0, keepdims=False)
            e_re, e_im = fields(p_re * spec_re - p_im * spec_im, p_re * spec_im + p_im * spec_re)
            place = offset + source
            store_re = lax.dynamic_update_index_in_dim(store_re, e_re, place, 0)
            store_im = lax.dynamic_update_index_in_dim(store_im, e_im, place, 0)
            return (total + src_scale[source] * (e_re * e_re + e_im * e_im), store_re, store_im)

        start = (jnp.zeros((tile, tile), jnp.float32), stores[0], stores[1])
        total, store_re, store_im = lax.fori_loop(
            zero_int, keeps[corner], forward_add_source, start
        )
        total, stores = (total, (store_re, store_im))
        partials.append(total)
        offset = offset + keeps[corner]
    partials = jnp.stack(partials)
    actives = (jnp.arange(corner_dev, dtype=jnp.int32) < own_load).astype(jnp.float32)
    summed = lax.psum(partials, "src")
    resist = jax.nn.sigmoid(resist_slope * (summed - resist_level))
    slopes = (
        2.0
        * (resist - target[None])
        * resist_slope
        * resist
        * (1.0 - resist)
        * actives[:, None, None]
    )
    gs_re = jnp.zeros((freqs, freqs), jnp.float32)
    gs_im = jnp.zeros((freqs, freqs), jnp.float32)
    for corner in range(corner_dev):
        corner_re = pup_re[:, corner]
        corner_im = pup_im[:, corner]
        adjoint_offset = offsets[corner]
        slope = slopes[corner]

        def adjoint_add_source(source, carry):
            place = adjoint_offset + source
            e_re = lax.dynamic_index_in_dim(stores[0], place, 0, keepdims=False)
            e_im = lax.dynamic_index_in_dim(stores[1], place, 0, keepdims=False)
            p_re = lax.dynamic_index_in_dim(corner_re, source, 0, keepdims=False)
            p_im = lax.dynamic_index_in_dim(corner_im, source, 0, keepdims=False)
            factor = 2.0 * src_scale[source] * slope
            ge_re = factor * e_re
            ge_im = factor * e_im
            gh_re = product(back_re_t, ge_re) + product(back_im_t, ge_im)
            gh_im = product(back_re_t, ge_im) - product(back_im_t, ge_re)
            gg_re = product(gh_re, back_re) + product(gh_im, back_im)
            gg_im = product(gh_im, back_re) - product(gh_re, back_im)
            return (carry[0] + p_re * gg_re + p_im * gg_im, carry[1] + p_re * gg_im - p_im * gg_re)

        empty = jnp.zeros((freqs, freqs), jnp.float32)
        part_re, part_im = lax.fori_loop(
            zero_int, keeps[corner], adjoint_add_source, (empty, empty)
        )
        gs_re = gs_re + part_re
        gs_im = gs_im + part_im
    gx_re = product(row_re.T, gs_re) + product(row_im.T, gs_im)
    gx_im = product(row_re.T, gs_im) - product(row_im.T, gs_re)
    window_grad = product(gx_re, col_re) + product(gx_im, col_im)
    from_right = passed_along(window_grad[:, :width], "tile", -1)
    from_left = passed_along(window_grad[:, width + tile :], "tile", 1)
    middle = add_edges(window_grad, width, tile, from_left, from_right)
    return lax.psum_scatter(middle, ("src", "focus"), scatter_dimension=0, tiled=True)


def solution(mesh):
    return jax.shard_map(
        per_device,
        mesh=mesh,
        in_specs=(
            P("parts", "tile"),
            P("parts", "tile"),
            P(None, "src", "focus", None, None),
            P("src"),
            P("parts"),
        ),
        out_specs=P(("parts", "src", "focus"), "tile"),
        check_vma=False,
    )
```

profile of v0, /device:TPU:0, one launch (start us, length us, event | category | flops | bytes accessed | tf_op | source)
XLA Modules:
  0.0 543.8 jit_solution(12759937555417626799)
XLA Ops:
  7.7 4.9 collective-permute-start
  18.0 2.9 collective-permute-done.1
  20.9 2.5 fusion.315
  24.1 2.5 fusion.316
  28.7 4.6 broadcast.89
  33.3 4.7 broadcast.89.clone
  38.0 97.6 %while.64 = (s32[]{:T(128)}, f32[384,384]{0,1:T(8,128)S(1)}, f32[16,384,384]{1,2,0:T(8,128)}, f32[16,384,384]{1,2,0:T(8,128)}, s32[]{:T(128)}, /*index=5*/f32[8]...) while((s32[]{:T(128)}, f32[384,384]{0,1:T(8,128)S(1)}, ...), condition=%wide.region_1.2_spmd.clone.clone.clone, body=%wide.region_0.1_spmd.clone.clone.clone.sunk | while | flops 532537344 | bytes 8239340 | solution.py:125
  42.5 2.4 bitcast_dynamic-update-slice_fusion.8
  47.1 2.5 fusion.505
  54.7 2.4 bitcast_dynamic-update-slice_fusion.8
  59.3 2.5 fusion.505
  66.8 2.4 bitcast_dynamic-update-slice_fusion.8
  71.4 2.5 fusion.505
  79.0 2.4 bitcast_dynamic-update-slice_fusion.8
  83.6 2.5 fusion.505
  91.2 2.4 bitcast_dynamic-update-slice_fusion.8
  95.7 2.5 fusion.505
  103.3 2.4 bitcast_dynamic-update-slice_fusion.8
  108.0 2.5 fusion.505
  115.5 2.4 bitcast_dynamic-update-slice_fusion.8
  120.1 2.5 fusion.505
  127.7 2.4 bitcast_dynamic-update-slice_fusion.8
  132.3 2.5 fusion.505
  137.6 9.7 %copy.10 = f32[16,384,384]{2,1,0:T(8,128)} copy(f32[16,384,384]{1,2,0:T(8,128)} %get-tuple-element.891) | data formatting | bytes 18874368
  147.3 9.7 %copy.11 = f32[16,384,384]{2,1,0:T(8,128)} copy(f32[16,384,384]{1,2,0:T(8,128)} %get-tuple-element.892) | data formatting | bytes 18874368
  157.0 119.7 %all-reduce.4.cloned.1.call-done = f32[2,384,384]{2,1,0:T(8,128)} async-done(((f32[2,384,384]{2,1,0:T(8,128)}), f32[2,384,384]{2,1,0:T(8,128)}) %all-reduce.4.cloned.1.call-update) | async-done | bytes 1179664 | tf_op jit(solution)/shard_map/psum | solution.py:133
  276.7 1.7 multiply_multiply_fusion
  279.0 114.6 %while.66 = (s32[]{:T(128)}, f32[64,64]{1,0:T(8,128)S(1)}, f32[64,64]{1,0:T(8,128)S(1)}, s32[]{:T(128)}, f32[8,64,64]{2,1,0:T(8,128)S(1)}, /*index=5*/f32[8]{0:T...) while((s32[]{:T(128)}, f32[64,64]{1,0:T(8,128)S(1)}, ...), condition=%wide.region_6.7_spmd.clone.clone.clone, body=%wide.region_5.6_spmd.clone.clone.clone.sunk | while | flops 532701184 | bytes 5914884 | solution.py:167
  286.0 2.0 fusion.524
  288.0 2.0 convolution_subtract_fusion.18
  291.1 2.0 fusion.526
  293.1 2.0 convolution_add_fusion.17
  299.6 2.0 fusion.524
  301.6 2.0 convolution_subtract_fusion.18
  304.7 2.0 fusion.526
  306.7 2.0 convolution_add_fusion.17
  313.2 2.0 fusion.524
  315.2 2.0 convolution_subtract_fusion.18
  318.3 2.0 fusion.526
  320.3 2.0 convolution_add_fusion.17
  326.8 2.0 fusion.524
  328.8 2.0 convolution_subtract_fusion.18
  331.9 2.0 fusion.526
  333.9 2.0 convolution_add_fusion.17
  340.4 2.0 fusion.524
  342.4 2.0 convolution_subtract_fusion.18
  345.5 2.0 fusion.526
  347.5 2.0 convolution_add_fusion.17
  354.0 2.0 fusion.524
  356.0 2.0 convolution_subtract_fusion.18
  359.1 2.0 fusion.526
  361.1 2.0 convolution_add_fusion.17
  367.6 2.0 fusion.524
  369.6 2.0 convolution_subtract_fusion.18
  372.7 2.0 fusion.526
  374.7 2.0 convolution_add_fusion.17
  381.2 2.0 fusion.524
  383.2 2.0 convolution_subtract_fusion.18
  386.3 2.0 fusion.526
  388.3 2.0 convolution_add_fusion.17
  400.0 3.4 collective-permute-start.2
  404.7 1.9 collective-permute-done.2
  406.6 107.2 %collective-permute-done.3 = f32[384,64]{1,0:T(8,128)S(1)} collective-permute-done((f32[384,64]{1,0:T(8,128)S(1)}, f32[384,64]{1,0:T(8,128)S(1)}, u32[]{:S(2)}, u32[]{:S(2)}) %collective-permute-start.3) | collective-permute-done | bytes 98336 | tf_op jit(solution)/shard_map/ppermute | solution.py:31
  514.9 21.8 %reduce-scatter.2.cloned.1.call-done = f32[96,384]{1,0:T(8,128)} async-done(((f32[384,384]{1,0:T(8,128)}), f32[96,384]{1,0:T(8,128)}) %reduce-scatter.2.cloned.1.call-update) | async-done | bytes 147472 | tf_op jit(solution)/shard_map/reduce_scatter | solution.py:178
  (155 shorter events, 116.7 us)
Async XLA Ops:
  6.5 270.1 %all-reduce.4.cloned.1.call-start = ((), (), s32[]{:S(2)}) async-start(), calls=%async_computation.1 | async-start | bytes 2359296 | tf_op jit(solution)/shard_map/psum | solution.py:133
  7.7 10.4 %collective-permute-start = (f32[384,64]{1,0:T(8,128)S(1)}, f32[384,64]{1,0:T(8,128)S(1)}, u32[]{:S(2)}, u32[]{:S(2)}) collective-permute-start(f32[384,64]{1,0:T(8,128)S(1)} %get-tuple-element.1018), channel_id=1, source_target_pairs={{0,4},{4,8},{8,12},{1,5},{5,9},{9,13},{2,6},{6,10},{10,14},{3,7},{... | collective-permute-start | bytes 294920 | tf_op jit(solution)/shard_map/ppermute | solution.py:20
  12.6 8.3 %collective-permute-start.1 = (f32[384,64]{1,0:T(8,128)S(1)}, f32[384,64]{1,0:T(8,128)S(1)}, u32[]{:S(2)}, u32[]{:S(2)}) collective-permute-start(f32[384,64]{1,0:T(8,128)S(1)} %get-tuple-element.1019), channel_id=1, source_target_pairs={{4,0},{8,4},{12,8},{5,1},{9,5},{13,9},{6,2},{10,6},{14,10},{7,3},{... | collective-permute-start | bytes 294920 | tf_op jit(solution)/shard_map/ppermute | solution.py:23
  137.6 399.2 %reduce-scatter.2.cloned.1.call-start = ((), (), s32[]{:S(2)}) async-start(), calls=%async_computation.2 | async-start | bytes 737280 | tf_op jit(solution)/shard_map/reduce_scatter | solution.py:178
  147.3 129.4 %copy-start = (f32[384,384]{1,0:T(8,128)S(1)}, f32[384,384]{1,0:T(8,128)}, u32[]{:S(2)}) copy-start(f32[384,384]{1,0:T(8,128)} %param.14) | copy-start | bytes 1769476
  400.0 6.6 %collective-permute-start.2 = (f32[384,64]{1,0:T(8,128)S(1)}, f32[384,64]{1,0:T(8,128)S(1)}, u32[]{:S(2)}, u32[]{:S(2)}) collective-permute-start(f32[384,64]{1,0:T(8,128)S(1)} %get-tuple-element.1016), channel_id=1, source_target_pairs={{0,4},{4,8},{8,12},{1,5},{5,9},{9,13},{2,6},{6,10},{10,14},{3,7},{... | collective-permute-start | bytes 294920 | tf_op jit(solution)/shard_map/ppermute | solution.py:31
  403.4 110.4 %collective-permute-start.3 = (f32[384,64]{1,0:T(8,128)S(1)}, f32[384,64]{1,0:T(8,128)S(1)}, u32[]{:S(2)}, u32[]{:S(2)}) collective-permute-start(f32[384,64]{1,0:T(8,128)S(1)} %get-tuple-element.1017), channel_id=1, source_target_pairs={{4,0},{8,4},{12,8},{5,1},{9,5},{13,9},{6,2},{10,6},{14,10},{7,3},{... | collective-permute-start | bytes 294920 | tf_op jit(solution)/shard_map/ppermute | solution.py:31
Sparse Core Ops, SparseCore 0:
  137.7 138.9 all-reduce.3
  515.0 21.6 reduce-scatter.1
where the time goes:
time: 553 us; the launch traced here: 544 us
  waiting for transfers between devices  253 us (46%)
  matrix products  196 us (35%)
  local copies, waits for them, and re-layouts  50.7 us (9%)
  between operations  14.5 us (3%)
  loops' own time  13.1 us (2%)
  starting transfers between devices  11 us (2%)
    dot_general x140, matrix products, product(): jnp.dot(left, right, precision=lax.Precision.HIGHEST, preferred_element_t...  196 us
    psum x1, waiting for transfers between devices, per_device(): summed = lax.psum(partials, 'src')  120 us
    ppermute x2, waiting for transfers between devices, passed_along(): return lax.ppermute(value, axis, pairs)  109 us
    reduce_scatter x1, waiting for transfers between devices, per_device(): lax.psum_scatter(middle, ('src', 'focus'), scatter_dimension=0, tiled=True)  21.8 us
    unnamed x4, local copies, waits for them, and re-layouts  19.3 us
    another operation x2, loops' own time, per_device(): lax.fori_loop(zero_int, keeps[corner], adjoint_add_source, (empty, empty))  12.1 us
  transfers between devices with their start and end apart: 6, of which 5 were waited for; matrix products, arithmetic and copies ran while one was open for 4% of the time, Pallas kernels for 0%

commit v1 on v0

v1 whole, which is shorter than its diff:
```python
import functools
import math

import jax
import jax.numpy as jnp
import ml_dtypes
import numpy as np
from jax import lax
from jax.experimental import pallas as pl
from jax.experimental.pallas import tpu as pltpu
from jax.sharding import PartitionSpec as P

AMBIT = 64
MESH = pl.DeviceIdType.MESH

resist_slope = 4.0
resist_level = 0.5


def halves(table):
    table = table.astype(np.float32)
    high = table.astype(ml_dtypes.bfloat16)
    low = (table - high.astype(np.float32)).astype(ml_dtypes.bfloat16)
    return high, low


def left_table(table):
    high, low = halves(table)
    return np.concatenate([high, low, high], axis=1)


def right_table(table):
    high, low = halves(table)
    return np.concatenate([high, low, high], axis=0)


def tables(tile, freqs, width):
    win = tile + 2 * width
    grid = 2 * freqs
    k = np.arange(freqs) - freqs // 2
    row = 2.0 * np.pi * ((k[:, None] * (np.arange(tile) + width)[None, :]) % win) / win
    row2 = np.concatenate([np.cos(row), -np.sin(row)], axis=0) / math.sqrt(win)
    col = 2.0 * np.pi * ((k[:, None] * np.arange(win)[None, :]) % win) / win
    col2 = np.concatenate([np.cos(col), -np.sin(col)], axis=0) / math.sqrt(win)
    own = col2[:, width : width + tile]
    to_left = np.zeros((2 * width, 2 * freqs))
    to_left[:width] = col2[:, width + tile :].T
    to_right = np.zeros((2 * width, 2 * freqs))
    to_right[width:] = col2[:, :width].T
    at = 2.0 * np.pi * ((k[:, None] * np.arange(grid)[None, :]) % grid) / grid
    c, s = np.cos(at) * math.sqrt(2.0 / freqs), np.sin(at) * math.sqrt(2.0 / freqs)
    field = np.block([[c, s], [-s, c]])
    q = np.arange(1 - freqs, freqs)
    gap = (np.arange(tile) + width)[:, None] / win - np.arange(grid)[None, :] / grid
    fine = np.cos(2.0 * np.pi * gap[:, :, None] * q[None, None, :]).sum(-1) / grid
    back = np.zeros((6 * freqs, tile))
    back[: 2 * freqs] = own
    back[2 * freqs : 4 * freqs, :width] = col2[:, width + tile :]
    back[4 * freqs :, tile - width :] = col2[:, :width]
    return dict(
        row=left_table(row2),
        own=right_table(own.T),
        to_left=right_table(to_left),
        to_right=right_table(to_right),
        f1r=right_table(field),
        f2l=left_table(field.T),
        f1l=left_table(field),
        f2r=right_table(field.T),
        ul=left_table(fine),
        utr=right_table(fine.T),
        ur=right_table(fine),
        utl=left_table(fine.T),
        rowt=left_table(row2.T),
        back=right_table(back),
    )


def split(x):
    high = x.astype(jnp.bfloat16)
    low = (x - high.astype(jnp.float32)).astype(jnp.bfloat16)
    return high, low


def dot(a, b):
    return jnp.dot(a, b, preferred_element_type=jnp.float32)


def times_table(x, table):
    high, low = split(x)
    return dot(jnp.concatenate([high, high, low], axis=1), table)


def table_times(table, x):
    high, low = split(x)
    return dot(table, jnp.concatenate([high, high, low], axis=0))


NAMES = (
    "row", "own", "to_left", "to_right", "f1r", "f2l", "f1l", "f2r",
    "ul", "utr", "ur", "utl", "rowt", "back",
)


def kernel(dims, counts_ref, w_ref, mask_ref, target_ref, pup_ref, *refs):
    ns, nf, nt, local_src, corners, freqs, tile = dims
    tab = dict(zip(NAMES, refs[: len(NAMES)]))
    (out_ref, p_ref, e_ref, zs_send, zs_recv, i_send, i_recv, g_send, g_recv, zg_send, zg_recv,
     zs_ss, zs_rs, i_ss, i_rs, g_ss, g_rs, zg_ss, zg_rs) = refs[len(NAMES):]
    grid = 2 * freqs
    rows = out_ref.shape[0]
    sources = local_src * ns
    t = lax.axis_index("tile")
    src = lax.axis_index("src")
    focus = lax.axis_index("focus")
    has_left = t > 0
    has_right = t < nt - 1
    left = {"tile": jnp.maximum(t - 1, 0)}
    right = {"tile": jnp.minimum(t + 1, nt - 1)}
    peers = [(a, b) for a in range(ns) for b in range(nf) if a + b > 0]

    def peer(a, b):
        return {"src": lax.rem(src + a, ns), "focus": lax.rem(focus + b, nf)}

    def remote(source, dest, ssem, rsem, device):
        return pltpu.make_async_remote_copy(
            src_ref=source, dst_ref=dest, send_sem=ssem, recv_sem=rsem,
            device_id=device, device_id_type=MESH,
        )

    def along(send, recv, ssem, rsem):
        return (
            remote(send.at[0], recv.at[1], ssem.at[0], rsem.at[1], left),
            remote(send.at[1], recv.at[0], ssem.at[1], rsem.at[0], right),
        )

    zs_recv[...] = jnp.zeros_like(zs_recv)
    zg_recv[...] = jnp.zeros_like(zg_recv)
    barrier = pltpu.get_barrier_semaphore()
    for a, b in peers:
        pl.semaphore_signal(barrier, inc=1, device_id=peer(a, b), device_id_type=MESH)

    @pl.when(has_left)
    def _():
        pl.semaphore_signal(barrier, inc=1, device_id=left, device_id_type=MESH)

    @pl.when(has_right)
    def _():
        pl.semaphore_signal(barrier, inc=1, device_id=right, device_id_type=MESH)

    lane = lax.broadcasted_iota(jnp.int32, (freqs, grid), 1)
    first = lane < freqs

    def swap(x):
        return pltpu.roll(x, freqs, 1)

    def complex_of(q):
        top, low = q[:freqs], swap(q[freqs:])
        return jnp.where(first, top - low, top + low)

    ah, al = split(table_times(tab["row"][...], mask_ref[...]))

    def columns(begin, end, table):
        high, low = ah[:, begin:end], al[:, begin:end]
        return complex_of(dot(jnp.concatenate([high, high, low], axis=1), table[...]))

    zs_send[0] = columns(0, 2 * AMBIT, tab["to_left"])
    zs_send[1] = columns(tile - 2 * AMBIT, tile, tab["to_right"])
    pl.semaphore_wait(
        barrier, len(peers) + has_left.astype(jnp.int32) + has_right.astype(jnp.int32)
    )
    zs_left, zs_right = along(zs_send, zs_recv, zs_ss, zs_rs)
    pl.when(has_left)(zs_left.start)
    pl.when(has_right)(zs_right.start)
    spec = columns(0, tile, tab["own"])
    for corner in range(corners):
        for s in range(local_src):
            p_ref[corner, s] = jnp.concatenate(
                [pup_ref[0, s, corner], pup_ref[1, s, corner]], axis=1
            )
    pl.when(has_left)(zs_right.wait_recv)
    pl.when(has_right)(zs_left.wait_recv)
    spec = spec + zs_recv[0] + zs_recv[1]
    turned = swap(spec)
    same = jnp.where(first, spec, turned)
    cross = jnp.where(first, -turned, spec)

    i_copies = []
    for corner in range(corners):
        parts = []
        for s in range(local_src):
            p = p_ref[corner, s]
            parts.append(p * same + swap(p) * cross)
        h = times_table(jnp.concatenate(parts, axis=0), tab["f1r"][...])
        h = jnp.concatenate(
            [
                jnp.concatenate(
                    [h[s * freqs : (s + 1) * freqs, :grid], h[s * freqs : (s + 1) * freqs, grid:]],
                    axis=0,
                )
                for s in range(local_src)
            ],
            axis=1,
        )
        e = table_times(tab["f2l"][...], h)
        e_ref[corner] = e
        total = jnp.zeros((grid, grid), jnp.float32)
        for s in range(local_src):
            e_re = e[:grid, s * grid : (s + 1) * grid]
            e_im = e[grid:, s * grid : (s + 1) * grid]
            total = total + (w_ref[s] * (1.0 / sources)) * (e_re * e_re + e_im * e_im)
        i_send[corner] = total
        for a in range(1, ns):
            copy = remote(
                i_send.at[corner], i_recv.at[a - 1, corner],
                i_ss.at[a - 1, corner], i_rs.at[a - 1, corner], peer(a, 0),
            )
            copy.start()
            i_copies.append(copy)

    count = counts_ref[t]
    sum_x = jnp.zeros((freqs, grid), jnp.float32)
    sum_y = jnp.zeros((freqs, grid), jnp.float32)
    for corner in range(corners):
        total = i_send[corner]
        for a in range(1, ns):
            i_copies[corner * (ns - 1) + a - 1].wait_recv()
            total = total + i_recv[a - 1, corner]
        intensity = times_table(table_times(tab["ul"][...], total), tab["utr"][...])
        decay = jnp.exp(-resist_slope * (intensity - resist_level))
        resist = 1.0 / (1.0 + decay)
        active = jnp.where(focus * corners + corner < count, 2.0 * resist_slope, 0.0)
        slope = active * (resist - target_ref[...]) * (decay * resist * resist)
        slope = table_times(tab["utl"][...], times_table(slope, tab["ur"][...]))
        slope = jnp.concatenate([slope, slope], axis=0)
        ge = jnp.concatenate(
            [e_ref[corner, :, s * grid : (s + 1) * grid] * slope for s in range(local_src)], axis=1
        )
        gh = table_times(tab["f1l"][...], ge)
        gh = jnp.concatenate(
            [
                jnp.concatenate(
                    [gh[:freqs, s * grid : (s + 1) * grid], gh[freqs:, s * grid : (s + 1) * grid]],
                    axis=1,
                )
                for s in range(local_src)
            ],
            axis=0,
        )
        gg = times_table(gh, tab["f2r"][...])
        for s in range(local_src):
            p = p_ref[corner, s]
            part = (w_ref[s] * (2.0 / sources)) * gg[s * freqs : (s + 1) * freqs]
            sum_x = sum_x + p * part
            sum_y = sum_y + swap(p) * part
    gs = jnp.where(first, sum_x + swap(sum_x), sum_y - swap(sum_y))

    g_send[...] = gs
    g_copies = []
    for n, (a, b) in enumerate(peers):
        copy = remote(g_send, g_recv.at[n], g_ss.at[n], g_rs.at[n], peer(a, b))
        copy.start()
        g_copies.append(copy)
    for n, copy in enumerate(g_copies):
        copy.wait_recv()
        gs = gs + g_recv[n]
    zg_send[0] = gs
    zg_send[1] = gs
    zg_left, zg_right = along(zg_send, zg_recv, zg_ss, zg_rs)
    pl.when(has_left)(zg_left.start)
    pl.when(has_right)(zg_right.start)

    def stacked(g):
        turned = swap(g)
        return jnp.concatenate([g, jnp.where(first, turned, -turned)], axis=0)

    begin = pl.multiple_of((src * nf + focus) * rows, 16)
    rowt = tab["rowt"][pl.ds(begin, rows), :]
    pl.when(has_left)(zg_right.wait_recv)
    pl.when(has_right)(zg_left.wait_recv)
    gx = table_times(
        rowt, jnp.concatenate([stacked(gs), stacked(zg_recv[0]), stacked(zg_recv[1])], axis=1)
    )
    out_ref[...] = times_table(gx, tab["back"][...])

    pl.when(has_left)(zs_left.wait_send)
    pl.when(has_right)(zs_right.wait_send)
    pl.when(has_left)(zg_left.wait_send)
    pl.when(has_right)(zg_right.wait_send)
    for copy in i_copies + g_copies:
        copy.wait_send()


def per_device(mask, target, pupil, weights, counts):
    tile = mask.shape[0]
    freqs = pupil.shape[-1]
    local_src = weights.shape[0]
    corners = pupil.shape[2]
    ns, nf, nt = (lax.axis_size(axis) for axis in ("src", "focus", "tile"))
    grid = 2 * freqs
    rows = tile // (ns * nf)
    peers = ns * nf - 1
    held = tables(tile, freqs, AMBIT)
    vmem = pl.BlockSpec(memory_space=pltpu.VMEM)
    smem = pl.BlockSpec(memory_space=pltpu.SMEM)
    f32 = jnp.float32
    dma = pltpu.SemaphoreType.DMA
    return pl.pallas_call(
        functools.partial(kernel, (ns, nf, nt, local_src, corners, freqs, tile)),
        out_shape=jax.ShapeDtypeStruct((rows, tile), f32),
        in_specs=[smem, smem] + [vmem] * (3 + len(NAMES)),
        out_specs=vmem,
        scratch_shapes=[
            pltpu.VMEM((corners, local_src, freqs, grid), f32),
            pltpu.VMEM((corners, 2 * grid, local_src * grid), f32),
            pltpu.VMEM((2, freqs, grid), f32),
            pltpu.VMEM((2, freqs, grid), f32),
            pltpu.VMEM((corners, grid, grid), f32),
            pltpu.VMEM((max(ns - 1, 1), corners, grid, grid), f32),
            pltpu.VMEM((freqs, grid), f32),
            pltpu.VMEM((max(peers, 1), freqs, grid), f32),
            pltpu.VMEM((2, freqs, grid), f32),
            pltpu.VMEM((2, freqs, grid), f32),
            dma((2,)),
            dma((2,)),
            dma((max(ns - 1, 1), corners)),
            dma((max(ns - 1, 1), corners)),
            dma((max(peers, 1),)),
            dma((max(peers, 1),)),
            dma((2,)),
            dma((2,)),
        ],
        compiler_params=pltpu.CompilerParams(
            collective_id=0, has_side_effects=True, vmem_limit_bytes=48 * 1024 * 1024
        ),
        name="abbe_gradient",
    )(counts, weights, mask, target, pupil, *[jnp.asarray(held[name]) for name in NAMES])


def solution(mesh):
    return jax.shard_map(
        per_device,
        mesh=mesh,
        in_specs=(
            P("parts", "tile"),
            P("parts", "tile"),
            P(None, "src", "focus", None, None),
            P("src"),
            P("parts"),
        ),
        out_specs=P(("parts", "src", "focus"), "tile"),
        check_vma=False,
    )
```

time: 553 us -> 42 us (0.08); the launches traced: 544 us -> 41.3 us
  waiting for transfers between devices: 253 us -> 0 us
  matrix products: 196 us -> 0 us
  local copies, waits for them, and re-layouts: 50.7 us -> 17.5 us
  Pallas kernels: 0 us -> 23.8 us
  between operations: 14.5 us -> 0.03 us
  loops' own time: 13.1 us -> 0 us
  starting transfers between devices: 11 us -> 0 us
    dot_general x140 -> x0, matrix products: 196 us -> none  [product(): jnp.dot(left, right, precision=lax.Precision.HIGHEST, preferred_element_t...]
    psum x1 -> x0, waiting for transfers between devices: 120 us -> none  [per_device(): summed = lax.psum(partials, 'src')]
    ppermute x4 -> x0, waiting for transfers between devices: 112 us -> none  [the longest x2 109 us: passed_along(): return lax.ppermute(value, axis, pairs)]
    pallas_call x0 -> x1, Pallas kernels: none -> 23.8 us  [per_device(): pl.pallas_call(functools.partial(kernel, (ns, nf, nt, local_src, corners,...]
    reduce_scatter x1 -> x0, waiting for transfers between devices: 21.8 us -> none  [per_device(): lax.psum_scatter(middle, ('src', 'focus'), scatter_dimension=0, tiled=True)]
    another operation x4 -> x0, loops' own time: 13.1 us -> none  [the longest x2 12.1 us: per_device(): lax.fori_loop(zero_int, keeps[corner], adjoint_add_source, (empty, empty))]
    dynamic_slice x17 -> x0, local copies, waits for them, and re-layouts: 11.7 us -> none  [the longest x8 5.26 us: forward_add_source(): src_scale[source] * (e_re * e_re + e_im * e_im)]
    ppermute x4 -> x0, starting transfers between devices: 10.9 us -> none  [the longest x1 4.94 us: with_halo(): lax.ppermute(lax.slice_in_dim(block, block.shape[dim] - width, None, axis...]
  transfers between devices with their start and end apart: 6 -> 0, of which waited for: 5 -> 0; matrix products, arithmetic and copies ran while one was open for 4% -> 0% of each run, Pallas kernels for 0% -> 0%
where the time goes in v1:
time: 42 us; the launch traced here: 41.3 us
  Pallas kernels  23.8 us (57%)
  local copies, waits for them, and re-layouts  17.5 us (42%)
    pallas_call x1, Pallas kernels, per_device(): pl.pallas_call(functools.partial(kernel, (ns, nf, nt, local_src, corners,...  23.8 us
    unnamed x37, local copies, waits for them, and re-layouts  17.5 us

profile of v1, /device:TPU:0, one launch (start us, length us, event | category | flops | bytes accessed | tf_op | source)
XLA Modules:
  0.0 41.3 jit_solution(4002980936423833389)
XLA Ops:
  0.0 0.0 copy-start
  0.0 1.2 %copy-done = bf16[1152,384]{1,0:T(8,128)(2,1)S(1)} copy-done((bf16[1152,384]{1,0:T(8,128)(2,1)S(1)}, bf16[1152,384]{1,0:T(8,128)(2,1)}, u32[]{:S(2)}) %copy-start) | copy-done | bytes 884760
  1.2 0.0 copy-start.1
  1.2 1.1 %copy-done.1 = f32[384,384]{1,0:T(8,128)S(1)} copy-done((f32[384,384]{1,0:T(8,128)S(1)}, f32[384,384]{1,0:T(8,128)}, u32[]{:S(2)}) %copy-start.1) | copy-done | bytes 589848
  2.2 0.0 copy-start.2
  2.2 1.1 %copy-done.2 = f32[384,384]{1,0:T(8,128)S(1)} copy-done((f32[384,384]{1,0:T(8,128)S(1)}, f32[384,384]{1,0:T(8,128)}, u32[]{:S(2)}) %copy-start.2) | copy-done | bytes 589848
  3.3 0.0 copy-start.3
  3.3 1.0 %copy-done.3 = bf16[384,384]{1,0:T(8,128)(2,1)S(1)} copy-done((bf16[384,384]{1,0:T(8,128)(2,1)S(1)}, bf16[384,384]{1,0:T(8,128)(2,1)}, u32[]{:S(2)}) %copy-start.3) | copy-done | bytes 294936
  4.3 0.0 copy-start.4
  4.3 1.0 %copy-done.4 = bf16[128,1152]{1,0:T(8,128)(2,1)S(1)} copy-done((bf16[128,1152]{1,0:T(8,128)(2,1)S(1)}, bf16[128,1152]{1,0:T(8,128)(2,1)}, u32[]{:S(2)}) %copy-start.4) | copy-done | bytes 294936
  5.2 0.0 copy-start.5
  5.2 1.0 %copy-done.5 = bf16[1152,128]{1,0:T(8,128)(2,1)S(1)} copy-done((bf16[1152,128]{1,0:T(8,128)(2,1)S(1)}, bf16[1152,128]{1,0:T(8,128)(2,1)}, u32[]{:S(2)}) %copy-start.5) | copy-done | bytes 294936
  6.2 0.0 copy-start.6
  6.2 1.0 %copy-done.6 = bf16[384,384]{1,0:T(8,128)(2,1)S(1)} copy-done((bf16[384,384]{1,0:T(8,128)(2,1)S(1)}, bf16[384,384]{1,0:T(8,128)(2,1)}, u32[]{:S(2)}) %copy-start.6) | copy-done | bytes 294936
  7.1 0.0 copy-start.7
  7.1 1.0 %copy-done.7 = bf16[384,384]{1,0:T(8,128)(2,1)S(1)} copy-done((bf16[384,384]{1,0:T(8,128)(2,1)S(1)}, bf16[384,384]{1,0:T(8,128)(2,1)}, u32[]{:S(2)}) %copy-start.7) | copy-done | bytes 294936
  8.1 0.0 copy-start.8
  8.1 1.0 %copy-done.8 = bf16[1152,128]{1,0:T(8,128)(2,1)S(1)} copy-done((bf16[1152,128]{1,0:T(8,128)(2,1)S(1)}, bf16[1152,128]{1,0:T(8,128)(2,1)}, u32[]{:S(2)}) %copy-start.8) | copy-done | bytes 294936
  9.1 0.0 copy-start.9
  9.1 1.0 %copy-done.9 = bf16[128,1152]{1,0:T(8,128)(2,1)S(1)} copy-done((bf16[128,1152]{1,0:T(8,128)(2,1)S(1)}, bf16[128,1152]{1,0:T(8,128)(2,1)}, u32[]{:S(2)}) %copy-start.9) | copy-done | bytes 294936
  10.0 0.0 copy-start.10
  10.0 0.9 %copy-done.10 = bf16[768,128]{1,0:T(8,128)(2,1)S(1)} copy-done((bf16[768,128]{1,0:T(8,128)(2,1)S(1)}, bf16[768,128]{1,0:T(8,128)(2,1)}, u32[]{:S(2)}) %copy-start.10) | copy-done | bytes 196632
  11.0 0.0 copy-start.11
  11.0 0.9 %copy-done.11 = bf16[128,768]{1,0:T(8,128)(2,1)S(1)} copy-done((bf16[128,768]{1,0:T(8,128)(2,1)S(1)}, bf16[128,768]{1,0:T(8,128)(2,1)}, u32[]{:S(2)}) %copy-start.11) | copy-done | bytes 196632
  11.9 0.0 copy-start.12
  11.9 0.9 %copy-done.12 = bf16[256,384]{1,0:T(8,128)(2,1)S(1)} copy-done((bf16[256,384]{1,0:T(8,128)(2,1)S(1)}, bf16[256,384]{1,0:T(8,128)(2,1)}, u32[]{:S(2)}) %copy-start.12) | copy-done | bytes 196632
  12.8 0.0 copy-start.13
  12.8 0.9 %copy-done.13 = bf16[384,256]{1,0:T(8,128)(2,1)S(1)} copy-done((bf16[384,256]{1,0:T(8,128)(2,1)S(1)}, bf16[384,256]{1,0:T(8,128)(2,1)}, u32[]{:S(2)}) %copy-start.13) | copy-done | bytes 196632
  13.7 0.0 copy-start.14
  13.7 0.9 %copy-done.14 = bf16[384,128]{1,0:T(8,128)(2,1)S(1)} copy-done((bf16[384,128]{1,0:T(8,128)(2,1)S(1)}, bf16[384,128]{1,0:T(8,128)(2,1)}, u32[]{:S(2)}) %copy-start.14) | copy-done | bytes 98328
  14.6 0.0 copy-start.15
  14.6 0.9 %copy-done.15 = bf16[384,128]{1,0:T(8,128)(2,1)S(1)} copy-done((bf16[384,128]{1,0:T(8,128)(2,1)S(1)}, bf16[384,128]{1,0:T(8,128)(2,1)}, u32[]{:S(2)}) %copy-start.15) | copy-done | bytes 98328
  15.5 0.0 copy-start.16
  15.5 0.7 %copy-done.16 = s32[4]{0:T(128)S(1)} copy-done((s32[4]{0:T(128)S(1)}, s32[4]{0:T(128)}, u32[]{:S(2)}) %copy-start.16) | copy-done | bytes 40
  16.2 0.0 copy-start.17
  16.2 0.7 %copy-done.17 = f32[8]{0:T(128)S(1)} copy-done((f32[8]{0:T(128)S(1)}, f32[8]{0:T(128)}, u32[]{:S(2)}) %copy-start.17) | copy-done | bytes 56
  16.8 23.8 %abbe_gradient.1 = f32[96,384]{1,0:T(8,128)S(1)} custom-call(s32[4]{0:T(128)S(1)} %copy-done.16, f32[8]{0:T(128)S(1)} %copy-done.17, f32[384,384]{1,0:T(8,128)S(1)} %copy-done.1, f32[384,384]{1,0:T(8,128)S(1)} %copy-done.2, f32[2,8,2,64,64]{4,3,2,1,0:T(8,128)} %pup_ref.1, bf16[128,1152]{1,0:T(8,128)(2,1)S(1)} %copy-done.9, bf16[1152,128]{1,0:T(8,128)(2,1)S(1)} %copy-done.8, ...), custom_call_target="tpu_custom_call" | custom-call | tf_op jit(solution)/shard_map/abbe_gradient/pallas_call | solution.py:307
  40.7 0.7 %copy.21 = f32[96,384]{1,0:T(8,128)} copy(f32[96,384]{1,0:T(8,128)S(1)} %abbe_gradient.1) | data formatting | bytes 294912
Async XLA Ops:
  0.0 1.2 %copy-start = (bf16[1152,384]{1,0:T(8,128)(2,1)S(1)}, bf16[1152,384]{1,0:T(8,128)(2,1)}, u32[]{:S(2)}) copy-start(bf16[1152,384]{1,0:T(8,128)(2,1)} %constant.41.clone.refs_13_) | copy-start | bytes 2654212
  1.2 1.1 %copy-start.1 = (f32[384,384]{1,0:T(8,128)S(1)}, f32[384,384]{1,0:T(8,128)}, u32[]{:S(2)}) copy-start(f32[384,384]{1,0:T(8,128)} %mask_ref.1) | copy-start | bytes 1769476
  2.2 1.1 %copy-start.2 = (f32[384,384]{1,0:T(8,128)S(1)}, f32[384,384]{1,0:T(8,128)}, u32[]{:S(2)}) copy-start(f32[384,384]{1,0:T(8,128)} %target_ref.1) | copy-start | bytes 1769476
  3.3 1.0 %copy-start.3 = (bf16[384,384]{1,0:T(8,128)(2,1)S(1)}, bf16[384,384]{1,0:T(8,128)(2,1)}, u32[]{:S(2)}) copy-start(bf16[384,384]{1,0:T(8,128)(2,1)} %constant.40.clone.refs_12_) | copy-start | bytes 884740
  4.3 1.0 %copy-start.4 = (bf16[128,1152]{1,0:T(8,128)(2,1)S(1)}, bf16[128,1152]{1,0:T(8,128)(2,1)}, u32[]{:S(2)}) copy-start(bf16[128,1152]{1,0:T(8,128)(2,1)} %constant.39.clone.refs_11_) | copy-start | bytes 884740
  5.2 1.0 %copy-start.5 = (bf16[1152,128]{1,0:T(8,128)(2,1)S(1)}, bf16[1152,128]{1,0:T(8,128)(2,1)}, u32[]{:S(2)}) copy-start(bf16[1152,128]{1,0:T(8,128)(2,1)} %constant.38.clone.refs_10_) | copy-start | bytes 884740
  6.2 1.0 %copy-start.6 = (bf16[384,384]{1,0:T(8,128)(2,1)S(1)}, bf16[384,384]{1,0:T(8,128)(2,1)}, u32[]{:S(2)}) copy-start(bf16[384,384]{1,0:T(8,128)(2,1)} %constant.37.clone.refs_9_) | copy-start | bytes 884740
  7.1 1.0 %copy-start.7 = (bf16[384,384]{1,0:T(8,128)(2,1)S(1)}, bf16[384,384]{1,0:T(8,128)(2,1)}, u32[]{:S(2)}) copy-start(bf16[384,384]{1,0:T(8,128)(2,1)} %constant.36.clone.refs_8_) | copy-start | bytes 884740
  8.1 1.0 %copy-start.8 = (bf16[1152,128]{1,0:T(8,128)(2,1)S(1)}, bf16[1152,128]{1,0:T(8,128)(2,1)}, u32[]{:S(2)}) copy-start(bf16[1152,128]{1,0:T(8,128)(2,1)} %constant.29.clone.refs_1_) | copy-start | bytes 884740
  9.1 1.0 %copy-start.9 = (bf16[128,1152]{1,0:T(8,128)(2,1)S(1)}, bf16[128,1152]{1,0:T(8,128)(2,1)}, u32[]{:S(2)}) copy-start(bf16[128,1152]{1,0:T(8,128)(2,1)} %constant.28.clone.refs_0_) | copy-start | bytes 884740
  10.0 0.9 %copy-start.10 = (bf16[768,128]{1,0:T(8,128)(2,1)S(1)}, bf16[768,128]{1,0:T(8,128)(2,1)}, u32[]{:S(2)}) copy-start(bf16[768,128]{1,0:T(8,128)(2,1)} %constant.35.clone.refs_7_) | copy-start | bytes 589828
  11.0 0.9 %copy-start.11 = (bf16[128,768]{1,0:T(8,128)(2,1)S(1)}, bf16[128,768]{1,0:T(8,128)(2,1)}, u32[]{:S(2)}) copy-start(bf16[128,768]{1,0:T(8,128)(2,1)} %constant.34.clone.refs_6_) | copy-start | bytes 589828
  11.9 0.9 %copy-start.12 = (bf16[256,384]{1,0:T(8,128)(2,1)S(1)}, bf16[256,384]{1,0:T(8,128)(2,1)}, u32[]{:S(2)}) copy-start(bf16[256,384]{1,0:T(8,128)(2,1)} %constant.33.clone.refs_5_) | copy-start | bytes 589828
  12.8 0.9 %copy-start.13 = (bf16[384,256]{1,0:T(8,128)(2,1)S(1)}, bf16[384,256]{1,0:T(8,128)(2,1)}, u32[]{:S(2)}) copy-start(bf16[384,256]{1,0:T(8,128)(2,1)} %constant.32.clone.refs_4_) | copy-start | bytes 589828
  13.7 0.9 %copy-start.14 = (bf16[384,128]{1,0:T(8,128)(2,1)S(1)}, bf16[384,128]{1,0:T(8,128)(2,1)}, u32[]{:S(2)}) copy-start(bf16[384,128]{1,0:T(8,128)(2,1)} %constant.31.clone.refs_3_) | copy-start | bytes 294916
  14.6 0.9 %copy-start.15 = (bf16[384,128]{1,0:T(8,128)(2,1)S(1)}, bf16[384,128]{1,0:T(8,128)(2,1)}, u32[]{:S(2)}) copy-start(bf16[384,128]{1,0:T(8,128)(2,1)} %constant.30.clone.refs_2_) | copy-start | bytes 294916
  15.5 0.7 %copy-start.16 = (s32[4]{0:T(128)S(1)}, s32[4]{0:T(128)}, u32[]{:S(2)}) copy-start(s32[4]{0:T(128)} %counts_ref.1) | copy-start | bytes 52
  16.2 0.7 %copy-start.17 = (f32[8]{0:T(128)S(1)}, f32[8]{0:T(128)}, u32[]{:S(2)}) copy-start(f32[8]{0:T(128)} %w_ref.1) | copy-start | bytes 100

commit v2 on v1

--- a/solution.py
+++ b/solution.py
@@ -21,17 +21,7 @@
     table = table.astype(np.float32)
     high = table.astype(ml_dtypes.bfloat16)
     low = (table - high.astype(np.float32)).astype(ml_dtypes.bfloat16)
-    return high, low
-
-
-def left_table(table):
-    high, low = halves(table)
-    return np.concatenate([high, low, high], axis=1)
-
-
-def right_table(table):
-    high, low = halves(table)
-    return np.concatenate([high, low, high], axis=0)
+    return np.stack([high, low])
 
 
 def tables(tile, freqs, width):
@@ -43,35 +33,25 @@
     col = 2.0 * np.pi * ((k[:, None] * np.arange(win)[None, :]) % win) / win
     col2 = np.concatenate([np.cos(col), -np.sin(col)], axis=0) / math.sqrt(win)
     own = col2[:, width : width + tile]
-    to_left = np.zeros((2 * width, 2 * freqs))
-    to_left[:width] = col2[:, width + tile :].T
-    to_right = np.zeros((2 * width, 2 * freqs))
-    to_right[width:] = col2[:, :width].T
+    edges = np.zeros((2, 2 * freqs, 2 * width))
+    edges[0, :, :width] = col2[:, width + tile :]
+    edges[1, :, width:] = col2[:, :width]
     at = 2.0 * np.pi * ((k[:, None] * np.arange(grid)[None, :]) % grid) / grid
     c, s = np.cos(at) * math.sqrt(2.0 / freqs), np.sin(at) * math.sqrt(2.0 / freqs)
     field = np.block([[c, s], [-s, c]])
     q = np.arange(1 - freqs, freqs)
     gap = (np.arange(tile) + width)[:, None] / win - np.arange(grid)[None, :] / grid
     fine = np.cos(2.0 * np.pi * gap[:, :, None] * q[None, None, :]).sum(-1) / grid
-    back = np.zeros((6 * freqs, tile))
-    back[: 2 * freqs] = own
-    back[2 * freqs : 4 * freqs, :width] = col2[:, width + tile :]
-    back[4 * freqs :, tile - width :] = col2[:, :width]
     return dict(
-        row=left_table(row2),
-        own=right_table(own.T),
-        to_left=right_table(to_left),
-        to_right=right_table(to_right),
-        f1r=right_table(field),
-        f2l=left_table(field.T),
-        f1l=left_table(field),
-        f2r=right_table(field.T),
-        ul=left_table(fine),
-        utr=right_table(fine.T),
-        ur=right_table(fine),
-        utl=left_table(fine.T),
-        rowt=left_table(row2.T),
-        back=right_table(back),
+        row=halves(row2),
+        own=halves(own),
+        left=halves(edges[0]),
+        right=halves(edges[1]),
+        f1=halves(field),
+        f2=halves(field.T),
+        fine=halves(fine),
+        finet=halves(fine.T),
+        rowt=halves(row2.T),
     )
 
 
@@ -85,27 +65,46 @@
     return jnp.dot(a, b, preferred_element_type=jnp.float32)
 
 
+def dot_t(a, b):
+    return lax.dot_general(a, b, (((1,), (1,)), ((), ())), preferred_element_type=jnp.float32)
+
+
 def times_table(x, table):
     high, low = split(x)
-    return dot(jnp.concatenate([high, high, low], axis=1), table)
+    return dot(
+        jnp.concatenate([high, high, low], axis=1),
+        jnp.concatenate([table[0], table[1], table[0]], axis=0),
+    )
+
+
+def times_turned(x, table):
+    high, low = split(x)
+    return dot_t(
+        jnp.concatenate([high, high, low], axis=1),
+        jnp.concatenate([table[0], table[1], table[0]], axis=1),
+    )
 
 
 def table_times(table, x):
     high, low = split(x)
-    return dot(table, jnp.concatenate([high, high, low], axis=0))
-
-
-NAMES = (
-    "row", "own", "to_left", "to_right", "f1r", "f2l", "f1l", "f2r",
-    "ul", "utr", "ur", "utl", "rowt", "back",
-)
-
-
-def kernel(dims, counts_ref, w_ref, mask_ref, target_ref, pup_ref, *refs):
+    return dot(
+        jnp.concatenate([table[0], table[1], table[0]], axis=1),
+        jnp.concatenate([high, high, low], axis=0),
+    )
+
+
+NAMES = ("row", "left", "right", "own", "f1", "f2", "fine", "finet", "rowt")
+
+
+def kernel(dims, counts_ref, w_ref, mask_hbm, target_hbm, pup_hbm, *refs):
     ns, nf, nt, local_src, corners, freqs, tile = dims
-    tab = dict(zip(NAMES, refs[: len(NAMES)]))
-    (out_ref, p_ref, e_ref, zs_send, zs_recv, i_send, i_recv, g_send, g_recv, zg_send, zg_recv,
-     zs_ss, zs_rs, i_ss, i_rs, g_ss, g_rs, zg_ss, zg_rs) = refs[len(NAMES):]
+    many = len(NAMES)
+    held = dict(zip(NAMES, refs[:many]))
+    out_ref = refs[many]
+    mask_ref, target_ref, pup_ref = refs[many + 1 : many + 4]
+    tab = dict(zip(NAMES, refs[many + 4 : 2 * many + 4]))
+    (load_sem, p_ref, e_ref, zs_send, zs_recv, i_send, i_recv, g_send, g_recv, zg_send, zg_recv,
+     zs_ss, zs_rs, i_ss, i_rs, g_ss, g_rs, zg_ss, zg_rs) = refs[2 * many + 4 :]
     grid = 2 * freqs
     rows = out_ref.shape[0]
     sources = local_src * ns
@@ -133,6 +132,28 @@
             remote(send.at[1], recv.at[0], ssem.at[1], rsem.at[0], right),
         )
 
+    begin = pl.multiple_of((src * nf + focus) * rows, 16)
+    loads = {}
+
+    def load(name, source, dest):
+        loads[name] = pltpu.make_async_copy(source, dest, load_sem.at[len(loads)])
+        loads[name].start()
+
+    load("row", held["row"], tab["row"])
+    load("mask", mask_hbm, mask_ref)
+    for name in ("left", "right", "own"):
+        load(name, held[name], tab[name])
+    load("pupil", pup_hbm, pup_ref)
+    for name in ("f1", "f2", "fine"):
+        load(name, held[name], tab[name])
+    load("target", target_hbm, target_ref)
+    load("finet", held["finet"], tab["finet"])
+    load("rowt", held["rowt"].at[:, pl.ds(begin, rows), :], tab["rowt"])
+
+    def need(*names):
+        for name in names:
+            loads[name].wait()
+
     zs_recv[...] = jnp.zeros_like(zs_recv)
     zg_recv[...] = jnp.zeros_like(zg_recv)
     barrier = pltpu.get_barrier_semaphore()
@@ -157,21 +178,25 @@
         top, low = q[:freqs], swap(q[freqs:])
         return jnp.where(first, top - low, top + low)
 
-    ah, al = split(table_times(tab["row"][...], mask_ref[...]))
+    need("row", "mask", "left", "right")
+    ah, al = split(table_times(tab["row"], mask_ref[...]))
 
     def columns(begin, end, table):
         high, low = ah[:, begin:end], al[:, begin:end]
-        return complex_of(dot(jnp.concatenate([high, high, low], axis=1), table[...]))
-
-    zs_send[0] = columns(0, 2 * AMBIT, tab["to_left"])
-    zs_send[1] = columns(tile - 2 * AMBIT, tile, tab["to_right"])
+        wide = jnp.concatenate([table[0], table[1], table[0]], axis=1)
+        return complex_of(dot_t(jnp.concatenate([high, high, low], axis=1), wide))
+
+    zs_send[0] = columns(0, 2 * AMBIT, tab["left"])
+    zs_send[1] = columns(tile - 2 * AMBIT, tile, tab["right"])
     pl.semaphore_wait(
         barrier, len(peers) + has_left.astype(jnp.int32) + has_right.astype(jnp.int32)
     )
     zs_left, zs_right = along(zs_send, zs_recv, zs_ss, zs_rs)
     pl.when(has_left)(zs_left.start)
     pl.when(has_right)(zs_right.start)
+    need("own")
     spec = columns(0, tile, tab["own"])
+    need("pupil")
     for corner in range(corners):
         for s in range(local_src):
             p_ref[corner, s] = jnp.concatenate(
@@ -184,13 +209,14 @@
     same = jnp.where(first, spec, turned)
     cross = jnp.where(first, -turned, spec)
 
+    need("f1", "f2")
     i_copies = []
     for corner in range(corners):
         parts = []
         for s in range(local_src):
             p = p_ref[corner, s]
             parts.append(p * same + swap(p) * cross)
-        h = times_table(jnp.concatenate(parts, axis=0), tab["f1r"][...])
+        h = times_table(jnp.concatenate(parts, axis=0), tab["f1"])
         h = jnp.concatenate(
             [
                 jnp.concatenate(
@@ -201,7 +227,7 @@
             ],
             axis=1,
         )
-        e = table_times(tab["f2l"][...], h)
+        e = table_times(tab["f2"], h)
         e_ref[corner] = e
         total = jnp.zeros((grid, grid), jnp.float32)
         for s in range(local_src):
@@ -217,6 +243,7 @@
             copy.start()
             i_copies.append(copy)
 
+    need("fine", "target", "finet", "rowt")
     count = counts_ref[t]
     sum_x = jnp.zeros((freqs, grid), jnp.float32)
     sum_y = jnp.zeros((freqs, grid), jnp.float32)
@@ -225,17 +252,17 @@
         for a in range(1, ns):
             i_copies[corner * (ns - 1) + a - 1].wait_recv()
             total = total + i_recv[a - 1, corner]
-        intensity = times_table(table_times(tab["ul"][...], total), tab["utr"][...])
+        intensity = times_turned(table_times(tab["fine"], total), tab["fine"])
         decay = jnp.exp(-resist_slope * (intensity - resist_level))
         resist = 1.0 / (1.0 + decay)
         active = jnp.where(focus * corners + corner < count, 2.0 * resist_slope, 0.0)
         slope = active * (resist - target_ref[...]) * (decay * resist * resist)
-        slope = table_times(tab["utl"][...], times_table(slope, tab["ur"][...]))
+        slope = table_times(tab["finet"], times_table(slope, tab["fine"]))
         slope = jnp.concatenate([slope, slope], axis=0)
         ge = jnp.concatenate(
             [e_ref[corner, :, s * grid : (s + 1) * grid] * slope for s in range(local_src)], axis=1
         )
-        gh = table_times(tab["f1l"][...], ge)
+        gh = table_times(tab["f1"], ge)
         gh = jnp.concatenate(
             [
                 jnp.concatenate(
@@ -246,7 +273,7 @@
             ],
             axis=0,
         )
-        gg = times_table(gh, tab["f2r"][...])
+        gg = times_turned(gh, tab["f1"])
         for s in range(local_src):
             p = p_ref[corner, s]
             part = (w_ref[s] * (2.0 / sources)) * gg[s * freqs : (s + 1) * freqs]
@@ -273,14 +300,21 @@
         turned = swap(g)
         return jnp.concatenate([g, jnp.where(first, turned, -turned)], axis=0)
 
-    begin = pl.multiple_of((src * nf + focus) * rows, 16)
-    rowt = tab["rowt"][pl.ds(begin, rows), :]
     pl.when(has_left)(zg_right.wait_recv)
     pl.when(has_right)(zg_left.wait_recv)
     gx = table_times(
-        rowt, jnp.concatenate([stacked(gs), stacked(zg_recv[0]), stacked(zg_recv[1])], axis=1)
-    )
-    out_ref[...] = times_table(gx, tab["back"][...])
+        tab["rowt"],
+        jnp.concatenate([stacked(gs), stacked(zg_recv[0]), stacked(zg_recv[1])], axis=1),
+    )
+    out = times_table(gx[:, :grid], tab["own"])
+    from_left = times_table(gx[:, grid : 2 * grid], tab["left"])
+    from_right = times_table(gx[:, 2 * grid :], tab["right"])
+    filler = jnp.zeros((rows, tile - 2 * AMBIT), jnp.float32)
+    out_ref[...] = (
+        out
+        + jnp.concatenate([from_left, filler], axis=1)
+        + jnp.concatenate([filler, from_right], axis=1)
+    )
 
     pl.when(has_left)(zs_left.wait_send)
     pl.when(has_right)(zs_right.wait_send)
@@ -300,16 +334,26 @@
     rows = tile // (ns * nf)
     peers = ns * nf - 1
     held = tables(tile, freqs, AMBIT)
+    held = {name: jnp.asarray(held[name]) for name in NAMES}
     vmem = pl.BlockSpec(memory_space=pltpu.VMEM)
     smem = pl.BlockSpec(memory_space=pltpu.SMEM)
+    hbm = pl.BlockSpec(memory_space=pltpu.HBM)
     f32 = jnp.float32
     dma = pltpu.SemaphoreType.DMA
     return pl.pallas_call(
         functools.partial(kernel, (ns, nf, nt, local_src, corners, freqs, tile)),
         out_shape=jax.ShapeDtypeStruct((rows, tile), f32),
-        in_specs=[smem, smem] + [vmem] * (3 + len(NAMES)),
+        in_specs=[smem, smem] + [hbm] * (3 + len(NAMES)),
         out_specs=vmem,
         scratch_shapes=[
+            pltpu.VMEM(mask.shape, f32),
+            pltpu.VMEM(target.shape, f32),
+            pltpu.VMEM(pupil.shape, f32),
+            *[
+                pltpu.VMEM((2, rows, grid) if name == "rowt" else held[name].shape, jnp.bfloat16)
+                for name in NAMES
+            ],
+            dma((len(NAMES) + 3,)),
             pltpu.VMEM((corners, local_src, freqs, grid), f32),
             pltpu.VMEM((corners, 2 * grid, local_src * grid), f32),
             pltpu.VMEM((2, freqs, grid), f32),
@@ -330,10 +374,10 @@
             dma((2,)),
         ],
         compiler_params=pltpu.CompilerParams(
-            collective_id=0, has_side_effects=True, vmem_limit_bytes=48 * 1024 * 1024
+            collective_id=0, has_side_effects=True, vmem_limit_bytes=64 * 1024 * 1024
         ),
         name="abbe_gradient",
-    )(counts, weights, mask, target, pupil, *[jnp.asarray(held[name]) for name in NAMES])
+    )(counts, weights, mask, target, pupil, *[held[name] for name in NAMES])
 
 
 def solution(mesh):

time: 42 us -> 25.6 us (0.61); the launches traced: 41.3 us -> 25.5 us
  local copies, waits for them, and re-layouts: 17.5 us -> 1.58 us
    unnamed x37 -> x1, local copies, waits for them, and re-layouts: 17.5 us -> 1.58 us
where the time goes in v2:
time: 25.6 us; the launch traced here: 25.5 us
  Pallas kernels  23.9 us (93%)
  local copies, waits for them, and re-layouts  1.58 us (6%)
    pallas_call x1, Pallas kernels, per_device(): pl.pallas_call(functools.partial(kernel, (ns, nf, nt, local_src, corners,...  23.9 us
    unnamed x1, local copies, waits for them, and re-layouts  1.58 us

profile of v2, /device:TPU:0, one launch (start us, length us, event | category | flops | bytes accessed | tf_op | source)
XLA Modules:
  0.0 25.5 jit_solution(1662331447739261065)
XLA Ops:
  0.0 23.9 %abbe_gradient.1 = f32[96,384]{1,0:T(8,128)} custom-call(s32[4]{0:T(128)} %counts_ref.1, f32[8]{0:T(128)} %w_ref.1, f32[384,384]{1,0:T(8,128)} %mask_hbm.1, f32[384,384]{1,0:T(8,128)} %target_hbm.1, f32[2,8,2,64,64]{4,3,2,1,0:T(8,128)} %pup_hbm.1, bf16[2,128,384]{2,1,0:T(8,128)(2,1)} %constant.16.clone.refs_0_.refs_3_, ...), custom_call_target="tpu_custom_call" | custom-call | tf_op jit(solution)/shard_map/abbe_gradient/pallas_call | solution.py:343
  23.9 1.6 %copy.16 = f32[96,384]{1,0:T(8,128)} copy(f32[96,384]{1,0:T(8,128)} %abbe_gradient.1) | data formatting | bytes 294912

commit v3 on v2

--- a/solution.py
+++ b/solution.py
@@ -103,8 +103,8 @@
     out_ref = refs[many]
     mask_ref, target_ref, pup_ref = refs[many + 1 : many + 4]
     tab = dict(zip(NAMES, refs[many + 4 : 2 * many + 4]))
-    (load_sem, p_ref, e_ref, zs_send, zs_recv, i_send, i_recv, g_send, g_recv, zg_send, zg_recv,
-     zs_ss, zs_rs, i_ss, i_rs, g_ss, g_rs, zg_ss, zg_rs) = refs[2 * many + 4 :]
+    (load_sem, p_ref, e_ref, zs_send, zs_recv, i_send, i_recv, g_send, g_recv, g_sum, g_all,
+     zs_ss, zs_rs, i_ss, i_rs, g_ss, g_rs, a_ss, a_rs) = refs[2 * many + 4 :]
     grid = 2 * freqs
     rows = out_ref.shape[0]
     sources = local_src * ns
@@ -113,23 +113,25 @@
     focus = lax.axis_index("focus")
     has_left = t > 0
     has_right = t < nt - 1
-    left = {"tile": jnp.maximum(t - 1, 0)}
-    right = {"tile": jnp.minimum(t + 1, nt - 1)}
-    peers = [(a, b) for a in range(ns) for b in range(nf) if a + b > 0]
+    left, right = jnp.maximum(t - 1, 0), jnp.minimum(t + 1, nt - 1)
+    group = [(a, b) for a in range(ns) for b in range(nf)]
+    peers = group[1:]
+    piece = freqs // len(group)
+
+    def moved(a, b):
+        return lax.rem(src + a, ns), lax.rem(focus + b, nf)
 
     def peer(a, b):
-        return {"src": lax.rem(src + a, ns), "focus": lax.rem(focus + b, nf)}
+        s, f = moved(a, b)
+        return {"src": s, "focus": f}
+
+    def across(a, b, tile_index):
+        return {"tile": tile_index, **peer(a, b)}
 
     def remote(source, dest, ssem, rsem, device):
         return pltpu.make_async_remote_copy(
             src_ref=source, dst_ref=dest, send_sem=ssem, recv_sem=rsem,
             device_id=device, device_id_type=MESH,
-        )
-
-    def along(send, recv, ssem, rsem):
-        return (
-            remote(send.at[0], recv.at[1], ssem.at[0], rsem.at[1], left),
-            remote(send.at[1], recv.at[0], ssem.at[1], rsem.at[0], right),
         )
 
     begin = pl.multiple_of((src * nf + focus) * rows, 16)
@@ -155,18 +157,19 @@
             loads[name].wait()
 
     zs_recv[...] = jnp.zeros_like(zs_recv)
-    zg_recv[...] = jnp.zeros_like(zg_recv)
+    g_all[...] = jnp.zeros_like(g_all)
     barrier = pltpu.get_barrier_semaphore()
     for a, b in peers:
         pl.semaphore_signal(barrier, inc=1, device_id=peer(a, b), device_id_type=MESH)
 
-    @pl.when(has_left)
-    def _():
-        pl.semaphore_signal(barrier, inc=1, device_id=left, device_id_type=MESH)
-
-    @pl.when(has_right)
-    def _():
-        pl.semaphore_signal(barrier, inc=1, device_id=right, device_id_type=MESH)
+    def greet(tile_index):
+        for a, b in group:
+            pl.semaphore_signal(
+                barrier, inc=1, device_id=across(a, b, tile_index), device_id_type=MESH
+            )
+
+    pl.when(has_left)(functools.partial(greet, left))
+    pl.when(has_right)(functools.partial(greet, right))
 
     lane = lax.broadcasted_iota(jnp.int32, (freqs, grid), 1)
     first = lane < freqs
@@ -189,9 +192,11 @@
     zs_send[0] = columns(0, 2 * AMBIT, tab["left"])
     zs_send[1] = columns(tile - 2 * AMBIT, tile, tab["right"])
     pl.semaphore_wait(
-        barrier, len(peers) + has_left.astype(jnp.int32) + has_right.astype(jnp.int32)
-    )
-    zs_left, zs_right = along(zs_send, zs_recv, zs_ss, zs_rs)
+        barrier,
+        len(peers) + len(group) * (has_left.astype(jnp.int32) + has_right.astype(jnp.int32)),
+    )
+    zs_left = remote(zs_send.at[0], zs_recv.at[1], zs_ss.at[0], zs_rs.at[1], {"tile": left})
+    zs_right = remote(zs_send.at[1], zs_recv.at[0], zs_ss.at[1], zs_rs.at[0], {"tile": right})
     pl.when(has_left)(zs_left.start)
     pl.when(has_right)(zs_right.start)
     need("own")
@@ -253,10 +258,9 @@
             i_copies[corner * (ns - 1) + a - 1].wait_recv()
             total = total + i_recv[a - 1, corner]
         intensity = times_turned(table_times(tab["fine"], total), tab["fine"])
-        decay = jnp.exp(-resist_slope * (intensity - resist_level))
-        resist = 1.0 / (1.0 + decay)
-        active = jnp.where(focus * corners + corner < count, 2.0 * resist_slope, 0.0)
-        slope = active * (resist - target_ref[...]) * (decay * resist * resist)
+        wave = jnp.tanh((0.5 * resist_slope) * (intensity - resist_level))
+        active = jnp.where(focus * corners + corner < count, 0.25 * resist_slope, 0.0)
+        slope = active * ((1.0 - 2.0 * target_ref[...]) + wave) * (1.0 - wave * wave)
         slope = table_times(tab["finet"], times_table(slope, tab["fine"]))
         slope = jnp.concatenate([slope, slope], axis=0)
         ge = jnp.concatenate(
@@ -282,29 +286,52 @@
     gs = jnp.where(first, sum_x + swap(sum_x), sum_y - swap(sum_y))
 
     g_send[...] = gs
+    mine = pl.multiple_of((src * nf + focus) * piece, 8)
     g_copies = []
     for n, (a, b) in enumerate(peers):
-        copy = remote(g_send, g_recv.at[n], g_ss.at[n], g_rs.at[n], peer(a, b))
+        to_src, to_focus = moved(a, b)
+        theirs = pl.multiple_of((to_src * nf + to_focus) * piece, 8)
+        copy = remote(
+            g_send.at[pl.ds(theirs, piece), :], g_recv.at[n], g_ss.at[n], g_rs.at[n], peer(a, b)
+        )
         copy.start()
         g_copies.append(copy)
+    part = g_send[pl.ds(mine, piece), :]
     for n, copy in enumerate(g_copies):
         copy.wait_recv()
-        gs = gs + g_recv[n]
-    zg_send[0] = gs
-    zg_send[1] = gs
-    zg_left, zg_right = along(zg_send, zg_recv, zg_ss, zg_rs)
-    pl.when(has_left)(zg_left.start)
-    pl.when(has_right)(zg_right.start)
+        part = part + g_recv[n]
+    g_sum[...] = part
+    g_all[0, pl.ds(mine, piece), :] = part
+
+    def finished(kind, n, device):
+        place = g_all.at[kind, pl.ds(mine, piece), :]
+        return remote(g_sum, place, a_ss.at[kind, n], a_rs.at[kind, n], device)
+
+    a_peers = [finished(0, n, peer(a, b)) for n, (a, b) in enumerate(group) if n > 0]
+    a_right = [finished(1, n, across(a, b, right)) for n, (a, b) in enumerate(group)]
+    a_left = [finished(2, n, across(a, b, left)) for n, (a, b) in enumerate(group)]
+
+    def every(copies, step):
+        def run():
+            for copy in copies:
+                getattr(copy, step)()
+
+        return run
+
+    pl.when(has_left)(every(a_left, "start"))
+    pl.when(has_right)(every(a_right, "start"))
+    every(a_peers, "start")()
 
     def stacked(g):
         turned = swap(g)
         return jnp.concatenate([g, jnp.where(first, turned, -turned)], axis=0)
 
-    pl.when(has_left)(zg_right.wait_recv)
-    pl.when(has_right)(zg_left.wait_recv)
+    every(a_peers, "wait_recv")()
+    pl.when(has_left)(every(a_right, "wait_recv"))
+    pl.when(has_right)(every(a_left, "wait_recv"))
     gx = table_times(
         tab["rowt"],
-        jnp.concatenate([stacked(gs), stacked(zg_recv[0]), stacked(zg_recv[1])], axis=1),
+        jnp.concatenate([stacked(g_all[n]) for n in range(3)], axis=1),
     )
     out = times_table(gx[:, :grid], tab["own"])
     from_left = times_table(gx[:, grid : 2 * grid], tab["left"])
@@ -318,9 +345,9 @@
 
     pl.when(has_left)(zs_left.wait_send)
     pl.when(has_right)(zs_right.wait_send)
-    pl.when(has_left)(zg_left.wait_send)
-    pl.when(has_right)(zg_right.wait_send)
-    for copy in i_copies + g_copies:
+    pl.when(has_left)(every(a_left, "wait_send"))
+    pl.when(has_right)(every(a_right, "wait_send"))
+    for copy in i_copies + g_copies + a_peers:
         copy.wait_send()
 
 
@@ -333,6 +360,7 @@
     grid = 2 * freqs
     rows = tile // (ns * nf)
     peers = ns * nf - 1
+    piece = freqs // (ns * nf)
     held = tables(tile, freqs, AMBIT)
     held = {name: jnp.asarray(held[name]) for name in NAMES}
     vmem = pl.BlockSpec(memory_space=pltpu.VMEM)
@@ -361,17 +389,17 @@
             pltpu.VMEM((corners, grid, grid), f32),
             pltpu.VMEM((max(ns - 1, 1), corners, grid, grid), f32),
             pltpu.VMEM((freqs, grid), f32),
-            pltpu.VMEM((max(peers, 1), freqs, grid), f32),
-            pltpu.VMEM((2, freqs, grid), f32),
-            pltpu.VMEM((2, freqs, grid), f32),
+            pltpu.VMEM((max(peers, 1), piece, grid), f32),
+            pltpu.VMEM((piece, grid), f32),
+            pltpu.VMEM((3, freqs, grid), f32),
             dma((2,)),
             dma((2,)),
             dma((max(ns - 1, 1), corners)),
             dma((max(ns - 1, 1), corners)),
             dma((max(peers, 1),)),
             dma((max(peers, 1),)),
-            dma((2,)),
-            dma((2,)),
+            dma((3, peers + 1)),
+            dma((3, peers + 1)),
         ],
         compiler_params=pltpu.CompilerParams(
             collective_id=0, has_side_effects=True, vmem_limit_bytes=64 * 1024 * 1024

time: 25.6 us -> 26.4 us (1.031)
  Pallas kernels: 23.9 us -> 24.7 us
    pallas_call x1, Pallas kernels: 23.9 us -> 24.7 us  [per_device(): pl.pallas_call(functools.partial(kernel, (ns, nf, nt, local_src, corners,...]
where the time goes in v3:
time: 26.4 us; the launch traced here: 26.3 us
  Pallas kernels  24.7 us (94%)
  local copies, waits for them, and re-layouts  1.58 us (6%)
    pallas_call x1, Pallas kernels, per_device(): pl.pallas_call(functools.partial(kernel, (ns, nf, nt, local_src, corners,...  24.7 us
    unnamed x1, local copies, waits for them, and re-layouts  1.58 us

profile of v3, /device:TPU:0, one launch (start us, length us, event | category | flops | bytes accessed | tf_op | source)
XLA Modules:
  0.0 26.3 jit_solution(5435790260950497795)
XLA Ops:
  0.0 24.7 %abbe_gradient.1 = f32[96,384]{1,0:T(8,128)} custom-call(s32[4]{0:T(128)} %counts_ref.1, f32[8]{0:T(128)} %w_ref.1, f32[384,384]{1,0:T(8,128)} %mask_hbm.1, f32[384,384]{1,0:T(8,128)} %target_hbm.1, f32[2,8,2,64,64]{4,3,2,1,0:T(8,128)} %pup_hbm.1, bf16[2,128,384]{2,1,0:T(8,128)(2,1)} %constant.16.clone.refs_0_.refs_3_, ...), custom_call_target="tpu_custom_call" | custom-call | tf_op jit(solution)/shard_map/abbe_gradient/pallas_call | solution.py:371
  24.7 1.6 %copy.16 = f32[96,384]{1,0:T(8,128)} copy(f32[96,384]{1,0:T(8,128)} %abbe_gradient.1) | data formatting | bytes 294912

commit v4 on v2

--- a/solution.py
+++ b/solution.py
@@ -253,10 +253,9 @@
             i_copies[corner * (ns - 1) + a - 1].wait_recv()
             total = total + i_recv[a - 1, corner]
         intensity = times_turned(table_times(tab["fine"], total), tab["fine"])
-        decay = jnp.exp(-resist_slope * (intensity - resist_level))
-        resist = 1.0 / (1.0 + decay)
-        active = jnp.where(focus * corners + corner < count, 2.0 * resist_slope, 0.0)
-        slope = active * (resist - target_ref[...]) * (decay * resist * resist)
+        wave = jnp.tanh((0.5 * resist_slope) * (intensity - resist_level))
+        active = jnp.where(focus * corners + corner < count, 0.25 * resist_slope, 0.0)
+        slope = active * ((1.0 - 2.0 * target_ref[...]) + wave) * (1.0 - wave * wave)
         slope = table_times(tab["finet"], times_table(slope, tab["fine"]))
         slope = jnp.concatenate([slope, slope], axis=0)
         ge = jnp.concatenate(
@@ -300,21 +299,18 @@
         turned = swap(g)
         return jnp.concatenate([g, jnp.where(first, turned, -turned)], axis=0)
 
+    out = times_table(table_times(tab["rowt"], stacked(gs)), tab["own"])
     pl.when(has_left)(zg_right.wait_recv)
     pl.when(has_right)(zg_left.wait_recv)
     gx = table_times(
-        tab["rowt"],
-        jnp.concatenate([stacked(gs), stacked(zg_recv[0]), stacked(zg_recv[1])], axis=1),
-    )
-    out = times_table(gx[:, :grid], tab["own"])
-    from_left = times_table(gx[:, grid : 2 * grid], tab["left"])
-    from_right = times_table(gx[:, 2 * grid :], tab["right"])
-    filler = jnp.zeros((rows, tile - 2 * AMBIT), jnp.float32)
-    out_ref[...] = (
-        out
-        + jnp.concatenate([from_left, filler], axis=1)
-        + jnp.concatenate([filler, from_right], axis=1)
-    )
+        tab["rowt"], jnp.concatenate([stacked(zg_recv[0]), stacked(zg_recv[1])], axis=1)
+    )
+    edge = 2 * AMBIT
+    from_left = times_table(gx[:, :grid], tab["left"])
+    from_right = times_table(gx[:, grid:], tab["right"])
+    out_ref[:, :edge] = out[:, :edge] + from_left
+    out_ref[:, edge : tile - edge] = out[:, edge : tile - edge]
+    out_ref[:, tile - edge :] = out[:, tile - edge :] + from_right
 
     pl.when(has_left)(zs_left.wait_send)
     pl.when(has_right)(zs_right.wait_send)

time: 25.6 us -> 25.5 us (level)
  no operation moved by 1% of the time
where the time goes in v4:
time: 25.5 us; the launch traced here: 25.3 us
  Pallas kernels  23.7 us (93%)
  local copies, waits for them, and re-layouts  1.58 us (6%)
    pallas_call x1, Pallas kernels, per_device(): pl.pallas_call(functools.partial(kernel, (ns, nf, nt, local_src, corners,...  23.7 us
    unnamed x1, local copies, waits for them, and re-layouts  1.58 us

profile of v4, /device:TPU:0, one launch (start us, length us, event | category | flops | bytes accessed | tf_op | source)
XLA Modules:
  0.0 25.3 jit_solution(17466869113294997084)
XLA Ops:
  0.0 23.7 %abbe_gradient.1 = f32[96,384]{1,0:T(8,128)} custom-call(s32[4]{0:T(128)} %counts_ref.1, f32[8]{0:T(128)} %w_ref.1, f32[384,384]{1,0:T(8,128)} %mask_hbm.1, f32[384,384]{1,0:T(8,128)} %target_hbm.1, f32[2,8,2,64,64]{4,3,2,1,0:T(8,128)} %pup_hbm.1, bf16[2,128,384]{2,1,0:T(8,128)(2,1)} %constant.16.clone.refs_0_.refs_3_, ...), custom_call_target="tpu_custom_call" | custom-call | tf_op jit(solution)/shard_map/abbe_gradient/pallas_call | solution.py:339
  23.7 1.6 %copy.16 = f32[96,384]{1,0:T(8,128)} copy(f32[96,384]{1,0:T(8,128)} %abbe_gradient.1) | data formatting | bytes 294912

commit v5 on v4

--- a/solution.py
+++ b/solution.py
@@ -103,8 +103,8 @@
     out_ref = refs[many]
     mask_ref, target_ref, pup_ref = refs[many + 1 : many + 4]
     tab = dict(zip(NAMES, refs[many + 4 : 2 * many + 4]))
-    (load_sem, p_ref, e_ref, zs_send, zs_recv, i_send, i_recv, g_send, g_recv, zg_send, zg_recv,
-     zs_ss, zs_rs, i_ss, i_rs, g_ss, g_rs, zg_ss, zg_rs) = refs[2 * many + 4 :]
+    (load_sem, p_ref, e_ref, zs_send, zs_recv, i_send, i_recv, g_send, g_recv, c_recv, g_half, g_all,
+     zs_ss, zs_rs, i_ss, i_rs, g_ss, g_rs, c_ss, c_rs, h_ss, h_rs) = refs[2 * many + 4 :]
     grid = 2 * freqs
     rows = out_ref.shape[0]
     sources = local_src * ns
@@ -113,23 +113,20 @@
     focus = lax.axis_index("focus")
     has_left = t > 0
     has_right = t < nt - 1
-    left = {"tile": jnp.maximum(t - 1, 0)}
-    right = {"tile": jnp.minimum(t + 1, nt - 1)}
-    peers = [(a, b) for a in range(ns) for b in range(nf) if a + b > 0]
-
-    def peer(a, b):
-        return {"src": lax.rem(src + a, ns), "focus": lax.rem(focus + b, nf)}
+    left, right = jnp.maximum(t - 1, 0), jnp.minimum(t + 1, nt - 1)
+    half = freqs // nf
+    mine = pl.multiple_of(focus * half, 8)
+
+    def chip(a):
+        return lax.rem(src + a, ns)
+
+    def core(b):
+        return lax.rem(focus + b, nf)
 
     def remote(source, dest, ssem, rsem, device):
         return pltpu.make_async_remote_copy(
             src_ref=source, dst_ref=dest, send_sem=ssem, recv_sem=rsem,
             device_id=device, device_id_type=MESH,
-        )
-
-    def along(send, recv, ssem, rsem):
-        return (
-            remote(send.at[0], recv.at[1], ssem.at[0], rsem.at[1], left),
-            remote(send.at[1], recv.at[0], ssem.at[1], rsem.at[0], right),
         )
 
     begin = pl.multiple_of((src * nf + focus) * rows, 16)
@@ -155,18 +152,23 @@
             loads[name].wait()
 
     zs_recv[...] = jnp.zeros_like(zs_recv)
-    zg_recv[...] = jnp.zeros_like(zg_recv)
+    c_recv[...] = jnp.zeros_like(c_recv)
     barrier = pltpu.get_barrier_semaphore()
-    for a, b in peers:
-        pl.semaphore_signal(barrier, inc=1, device_id=peer(a, b), device_id_type=MESH)
-
-    @pl.when(has_left)
-    def _():
-        pl.semaphore_signal(barrier, inc=1, device_id=left, device_id_type=MESH)
-
-    @pl.when(has_right)
-    def _():
-        pl.semaphore_signal(barrier, inc=1, device_id=right, device_id_type=MESH)
+
+    def greet(device):
+        pl.semaphore_signal(barrier, inc=1, device_id=device, device_id_type=MESH)
+
+    for b in range(1, nf):
+        greet({"focus": core(b)})
+    for a in range(1, ns):
+        greet({"src": chip(a)})
+
+    def greet_tile(tile_index):
+        for a in range(ns):
+            greet({"tile": tile_index, "src": chip(a)})
+
+    pl.when(has_left)(functools.partial(greet_tile, left))
+    pl.when(has_right)(functools.partial(greet_tile, right))
 
     lane = lax.broadcasted_iota(jnp.int32, (freqs, grid), 1)
     first = lane < freqs
@@ -189,9 +191,11 @@
     zs_send[0] = columns(0, 2 * AMBIT, tab["left"])
     zs_send[1] = columns(tile - 2 * AMBIT, tile, tab["right"])
     pl.semaphore_wait(
-        barrier, len(peers) + has_left.astype(jnp.int32) + has_right.astype(jnp.int32)
-    )
-    zs_left, zs_right = along(zs_send, zs_recv, zs_ss, zs_rs)
+        barrier,
+        (ns + nf - 2) + ns * (has_left.astype(jnp.int32) + has_right.astype(jnp.int32)),
+    )
+    zs_left = remote(zs_send.at[0], zs_recv.at[1], zs_ss.at[0], zs_rs.at[1], {"tile": left})
+    zs_right = remote(zs_send.at[1], zs_recv.at[0], zs_ss.at[1], zs_rs.at[0], {"tile": right})
     pl.when(has_left)(zs_left.start)
     pl.when(has_right)(zs_right.start)
     need("own")
@@ -238,7 +242,7 @@
         for a in range(1, ns):
             copy = remote(
                 i_send.at[corner], i_recv.at[a - 1, corner],
-                i_ss.at[a - 1, corner], i_rs.at[a - 1, corner], peer(a, 0),
+                i_ss.at[a - 1, corner], i_rs.at[a - 1, corner], {"src": chip(a)},
             )
             copy.start()
             i_copies.append(copy)
@@ -280,31 +284,72 @@
             sum_y = sum_y + swap(p) * part
     gs = jnp.where(first, sum_x + swap(sum_x), sum_y - swap(sum_y))
 
+    def every(copies, step):
+        def run():
+            for copy in copies:
+                getattr(copy, step)()
+
+        return run
+
     g_send[...] = gs
     g_copies = []
-    for n, (a, b) in enumerate(peers):
-        copy = remote(g_send, g_recv.at[n], g_ss.at[n], g_rs.at[n], peer(a, b))
-        copy.start()
-        g_copies.append(copy)
-    for n, copy in enumerate(g_copies):
+    for b in range(1, nf):
+        theirs = pl.multiple_of(core(b) * half, 8)
+        g_copies.append(
+            remote(
+                g_send.at[pl.ds(theirs, half), :], g_recv.at[b - 1],
+                g_ss.at[b - 1], g_rs.at[b - 1], {"focus": core(b)},
+            )
+        )
+    every(g_copies, "start")()
+    part = g_send[pl.ds(mine, half), :]
+    for b, copy in enumerate(g_copies):
         copy.wait_recv()
-        gs = gs + g_recv[n]
-    zg_send[0] = gs
-    zg_send[1] = gs
-    zg_left, zg_right = along(zg_send, zg_recv, zg_ss, zg_rs)
-    pl.when(has_left)(zg_left.start)
-    pl.when(has_right)(zg_right.start)
+        part = part + g_recv[b]
+    c_recv[0, 0] = part
+
+    def onward(kind, a, device):
+        return remote(
+            c_recv.at[0, 0], c_recv.at[kind, a], c_ss.at[kind, a], c_rs.at[kind, a],
+            {"src": chip(a), **device},
+        )
+
+    chips = range(ns - 1, -1, -1)
+    c_peers = [onward(0, a, {}) for a in chips if a > 0]
+    c_right = [onward(1, a, {"tile": right}) for a in chips]
+    c_left = [onward(2, a, {"tile": left}) for a in chips]
+    pl.when(has_left)(every(c_left, "start"))
+    pl.when(has_right)(every(c_right, "start"))
+    every(c_peers, "start")()
+    every(c_peers, "wait_recv")()
+    pl.when(has_left)(every(c_right, "wait_recv"))
+    pl.when(has_right)(every(c_left, "wait_recv"))
+    for kind in range(3):
+        total = c_recv[kind, 0]
+        for a in range(1, ns):
+            total = total + c_recv[kind, a]
+        g_half[kind] = total
+        g_all[kind, pl.ds(mine, half), :] = total
+
+    h_copies = [
+        remote(
+            g_half, g_all.at[:, pl.ds(mine, half), :],
+            h_ss.at[b - 1], h_rs.at[b - 1], {"focus": core(b)},
+        )
+        for b in range(1, nf)
+    ]
+    every(h_copies, "start")()
 
     def stacked(g):
         turned = swap(g)
         return jnp.concatenate([g, jnp.where(first, turned, -turned)], axis=0)
 
-    out = times_table(table_times(tab["rowt"], stacked(gs)), tab["own"])
-    pl.when(has_left)(zg_right.wait_recv)
-    pl.when(has_right)(zg_left.wait_recv)
+    every(h_copies, "wait_recv")()
     gx = table_times(
-        tab["rowt"], jnp.concatenate([stacked(zg_recv[0]), stacked(zg_recv[1])], axis=1)
-    )
+        tab["rowt"], jnp.concatenate([stacked(g_all[kind]) for kind in range(3)], axis=1)
+    )
+    out = times_table(gx[:, :grid], tab["own"])
+    gx = gx[:, grid:]
     edge = 2 * AMBIT
     from_left = times_table(gx[:, :grid], tab["left"])
     from_right = times_table(gx[:, grid:], tab["right"])
@@ -314,9 +359,9 @@
 
     pl.when(has_left)(zs_left.wait_send)
     pl.when(has_right)(zs_right.wait_send)
-    pl.when(has_left)(zg_left.wait_send)
-    pl.when(has_right)(zg_right.wait_send)
-    for copy in i_copies + g_copies:
+    pl.when(has_left)(every(c_left, "wait_send"))
+    pl.when(has_right)(every(c_right, "wait_send"))
+    for copy in i_copies + g_copies + c_peers + h_copies:
         copy.wait_send()
 
 
@@ -328,7 +373,7 @@
     ns, nf, nt = (lax.axis_size(axis) for axis in ("src", "focus", "tile"))
     grid = 2 * freqs
     rows = tile // (ns * nf)
-    peers = ns * nf - 1
+    half = freqs // nf
     held = tables(tile, freqs, AMBIT)
     held = {name: jnp.asarray(held[name]) for name in NAMES}
     vmem = pl.BlockSpec(memory_space=pltpu.VMEM)
@@ -357,17 +402,20 @@
             pltpu.VMEM((corners, grid, grid), f32),
             pltpu.VMEM((max(ns - 1, 1), corners, grid, grid), f32),
             pltpu.VMEM((freqs, grid), f32),
-            pltpu.VMEM((max(peers, 1), freqs, grid), f32),
-            pltpu.VMEM((2, freqs, grid), f32),
-            pltpu.VMEM((2, freqs, grid), f32),
+            pltpu.VMEM((max(nf - 1, 1), half, grid), f32),
+            pltpu.VMEM((3, ns, half, grid), f32),
+            pltpu.VMEM((3, half, grid), f32),
+            pltpu.VMEM((3, freqs, grid), f32),
             dma((2,)),
             dma((2,)),
             dma((max(ns - 1, 1), corners)),
             dma((max(ns - 1, 1), corners)),
-            dma((max(peers, 1),)),
-            dma((max(peers, 1),)),
-            dma((2,)),
-            dma((2,)),
+            dma((max(nf - 1, 1),)),
+            dma((max(nf - 1, 1),)),
+            dma((3, ns)),
+            dma((3, ns)),
+            dma((max(nf - 1, 1),)),
+            dma((max(nf - 1, 1),)),
         ],
         compiler_params=pltpu.CompilerParams(
             collective_id=0, has_side_effects=True, vmem_limit_bytes=64 * 1024 * 1024

time: 25.5 us -> 24.9 us (0.976)
  Pallas kernels: 23.7 us -> 23.1 us
    pallas_call x1, Pallas kernels: 23.7 us -> 23.1 us  [per_device(): pl.pallas_call(functools.partial(kernel, (ns, nf, nt, local_src, corners,...]
where the time goes in v5:
time: 24.9 us; the launch traced here: 24.7 us
  Pallas kernels  23.1 us (93%)
  local copies, waits for them, and re-layouts  1.58 us (6%)
    pallas_call x1, Pallas kernels, per_device(): pl.pallas_call(functools.partial(kernel, (ns, nf, nt, local_src, corners,...  23.1 us
    unnamed x1, local copies, waits for them, and re-layouts  1.58 us

profile of v5, /device:TPU:0, one launch (start us, length us, event | category | flops | bytes accessed | tf_op | source)
XLA Modules:
  0.0 24.7 jit_solution(11629049953171120040)
XLA Ops:
  0.0 23.1 %abbe_gradient.1 = f32[96,384]{1,0:T(8,128)} custom-call(s32[4]{0:T(128)} %counts_ref.1, f32[8]{0:T(128)} %w_ref.1, f32[384,384]{1,0:T(8,128)} %mask_hbm.1, f32[384,384]{1,0:T(8,128)} %target_hbm.1, f32[2,8,2,64,64]{4,3,2,1,0:T(8,128)} %pup_hbm.1, bf16[2,128,384]{2,1,0:T(8,128)(2,1)} %constant.16.clone.refs_0_.refs_3_, ...), custom_call_target="tpu_custom_call" | custom-call | tf_op jit(solution)/shard_map/abbe_gradient/pallas_call | solution.py:384
  23.1 1.6 %copy.16 = f32[96,384]{1,0:T(8,128)} copy(f32[96,384]{1,0:T(8,128)} %abbe_gradient.1) | data formatting | bytes 294912

commit v6 on v5

--- a/solution.py
+++ b/solution.py
@@ -93,6 +93,12 @@
     )
 
 
+def narrow(high, low, table_high, table_low, axis, product):
+    size = table_high.shape[axis]
+    both = product(high, jnp.concatenate([table_high, table_low], axis=axis))
+    return both[:, :size] + (both[:, size:] + product(low, table_high))
+
+
 NAMES = ("row", "left", "right", "own", "f1", "f2", "fine", "finet", "rowt")
 
 
@@ -138,8 +144,44 @@
 
     load("row", held["row"], tab["row"])
     load("mask", mask_hbm, mask_ref)
-    for name in ("left", "right", "own"):
+    for name in ("left", "right"):
         load(name, held[name], tab[name])
+
+    def need(*names):
+        for name in names:
+            loads[name].wait()
+
+    zs_recv[...] = jnp.zeros_like(zs_recv)
+    c_recv[...] = jnp.zeros_like(c_recv)
+    barrier = pltpu.get_barrier_semaphore()
+
+    def greet(device):
+        pl.semaphore_signal(barrier, inc=1, device_id=device, device_id_type=MESH)
+
+    for b in range(1, nf):
+        greet({"focus": core(b)})
+    for a in range(1, ns):
+        greet({"src": chip(a)})
+
+    def greet_tile(tile_index):
+        for a in range(ns):
+            greet({"tile": tile_index, "src": chip(a)})
+
+    pl.when(has_left)(functools.partial(greet_tile, left))
+    pl.when(has_right)(functools.partial(greet_tile, right))
+
+    lane = lax.broadcasted_iota(jnp.int32, (freqs, grid), 1)
+    first = lane < freqs
+
+    def swap(x):
+        return pltpu.roll(x, freqs, 1)
+
+    def complex_of(q):
+        top, low = q[:freqs], swap(q[freqs:])
+        return jnp.where(first, top - low, top + low)
+
+    need("row", "mask", "left", "right")
+    load("own", held["own"], tab["own"])
     load("pupil", pup_hbm, pup_ref)
     for name in ("f1", "f2", "fine"):
         load(name, held[name], tab[name])
@@ -147,49 +189,16 @@
     load("finet", held["finet"], tab["finet"])
     load("rowt", held["rowt"].at[:, pl.ds(begin, rows), :], tab["rowt"])
 
-    def need(*names):
-        for name in names:
-            loads[name].wait()
-
-    zs_recv[...] = jnp.zeros_like(zs_recv)
-    c_recv[...] = jnp.zeros_like(c_recv)
-    barrier = pltpu.get_barrier_semaphore()
-
-    def greet(device):
-        pl.semaphore_signal(barrier, inc=1, device_id=device, device_id_type=MESH)
-
-    for b in range(1, nf):
-        greet({"focus": core(b)})
-    for a in range(1, ns):
-        greet({"src": chip(a)})
-
-    def greet_tile(tile_index):
-        for a in range(ns):
-            greet({"tile": tile_index, "src": chip(a)})
-
-    pl.when(has_left)(functools.partial(greet_tile, left))
-    pl.when(has_right)(functools.partial(greet_tile, right))
-
-    lane = lax.broadcasted_iota(jnp.int32, (freqs, grid), 1)
-    first = lane < freqs
-
-    def swap(x):
-        return pltpu.roll(x, freqs, 1)
-
-    def complex_of(q):
-        top, low = q[:freqs], swap(q[freqs:])
-        return jnp.where(first, top - low, top + low)
-
-    need("row", "mask", "left", "right")
-    ah, al = split(table_times(tab["row"], mask_ref[...]))
-
-    def columns(begin, end, table):
-        high, low = ah[:, begin:end], al[:, begin:end]
+    edge = 2 * AMBIT
+
+    def columns(high, low, table):
         wide = jnp.concatenate([table[0], table[1], table[0]], axis=1)
         return complex_of(dot_t(jnp.concatenate([high, high, low], axis=1), wide))
 
-    zs_send[0] = columns(0, 2 * AMBIT, tab["left"])
-    zs_send[1] = columns(tile - 2 * AMBIT, tile, tab["right"])
+    sides = jnp.concatenate([mask_ref[:, :edge], mask_ref[:, tile - edge :]], axis=1)
+    sh, sl = split(table_times(tab["row"], sides))
+    zs_send[0] = columns(sh[:, :edge], sl[:, :edge], tab["left"])
+    zs_send[1] = columns(sh[:, edge:], sl[:, edge:], tab["right"])
     pl.semaphore_wait(
         barrier,
         (ns + nf - 2) + ns * (has_left.astype(jnp.int32) + has_right.astype(jnp.int32)),
@@ -198,8 +207,13 @@
     zs_right = remote(zs_send.at[1], zs_recv.at[0], zs_ss.at[1], zs_rs.at[0], {"tile": right})
     pl.when(has_left)(zs_left.start)
     pl.when(has_right)(zs_right.start)
+    mh, ml = split(table_times(tab["row"], mask_ref[:, edge : tile - edge]))
     need("own")
-    spec = columns(0, tile, tab["own"])
+    spec = columns(
+        jnp.concatenate([sh[:, :edge], mh, sh[:, edge:]], axis=1),
+        jnp.concatenate([sl[:, :edge], ml, sl[:, edge:]], axis=1),
+        tab["own"],
+    )
     need("pupil")
     for corner in range(corners):
         for s in range(local_src):
@@ -260,7 +274,8 @@
         wave = jnp.tanh((0.5 * resist_slope) * (intensity - resist_level))
         active = jnp.where(focus * corners + corner < count, 0.25 * resist_slope, 0.0)
         slope = active * ((1.0 - 2.0 * target_ref[...]) + wave) * (1.0 - wave * wave)
-        slope = table_times(tab["finet"], times_table(slope, tab["fine"]))
+        slope = narrow(*split(slope), tab["fine"][0], tab["fine"][1], 1, dot)
+        slope = narrow(tab["finet"][0], tab["finet"][1], *split(slope), 1, dot)
         slope = jnp.concatenate([slope, slope], axis=0)
         ge = jnp.concatenate(
             [e_ref[corner, :, s * grid : (s + 1) * grid] * slope for s in range(local_src)], axis=1
@@ -276,7 +291,7 @@
             ],
             axis=0,
         )
-        gg = times_turned(gh, tab["f1"])
+        gg = narrow(*split(gh), tab["f1"][0], tab["f1"][1], 0, dot_t)
         for s in range(local_src):
             p = p_ref[corner, s]
             part = (w_ref[s] * (2.0 / sources)) * gg[s * freqs : (s + 1) * freqs]
@@ -350,7 +365,6 @@
     )
     out = times_table(gx[:, :grid], tab["own"])
     gx = gx[:, grid:]
-    edge = 2 * AMBIT
     from_left = times_table(gx[:, :grid], tab["left"])
     from_right = times_table(gx[:, grid:], tab["right"])
     out_ref[:, :edge] = out[:, :edge] + from_left

time: 24.9 us -> 23.7 us (0.952)
  Pallas kernels: 23.1 us -> 21.9 us
    pallas_call x1, Pallas kernels: 23.1 us -> 21.9 us  [per_device(): pl.pallas_call(functools.partial(kernel, (ns, nf, nt, local_src, corners,...]
where the time goes in v6:
time: 23.7 us; the launch traced here: 23.5 us
  Pallas kernels  21.9 us (92%)
  local copies, waits for them, and re-layouts  1.58 us (7%)
    pallas_call x1, Pallas kernels, per_device(): pl.pallas_call(functools.partial(kernel, (ns, nf, nt, local_src, corners,...  21.9 us
    unnamed x1, local copies, waits for them, and re-layouts  1.58 us

profile of v6, /device:TPU:0, one launch (start us, length us, event | category | flops | bytes accessed | tf_op | source)
XLA Modules:
  0.0 23.5 jit_solution(9467347956570274927)
XLA Ops:
  0.0 21.9 %abbe_gradient.1 = f32[96,384]{1,0:T(8,128)} custom-call(s32[4]{0:T(128)} %counts_ref.1, f32[8]{0:T(128)} %w_ref.1, f32[384,384]{1,0:T(8,128)} %mask_hbm.1, f32[384,384]{1,0:T(8,128)} %target_hbm.1, f32[2,8,2,64,64]{4,3,2,1,0:T(8,128)} %pup_hbm.1, bf16[2,128,384]{2,1,0:T(8,128)(2,1)} %constant.16.clone.refs_0_.refs_3_, ...), custom_call_target="tpu_custom_call" | custom-call | tf_op jit(solution)/shard_map/abbe_gradient/pallas_call | solution.py:398
  22.0 1.6 %copy.16 = f32[96,384]{1,0:T(8,128)} copy(f32[96,384]{1,0:T(8,128)} %abbe_gradient.1) | data formatting | bytes 294912

commit v7 on v6

--- a/solution.py
+++ b/solution.py
@@ -265,6 +265,7 @@
     count = counts_ref[t]
     sum_x = jnp.zeros((freqs, grid), jnp.float32)
     sum_y = jnp.zeros((freqs, grid), jnp.float32)
+    slopes = []
     for corner in range(corners):
         total = i_send[corner]
         for a in range(1, ns):
@@ -276,7 +277,8 @@
         slope = active * ((1.0 - 2.0 * target_ref[...]) + wave) * (1.0 - wave * wave)
         slope = narrow(*split(slope), tab["fine"][0], tab["fine"][1], 1, dot)
         slope = narrow(tab["finet"][0], tab["finet"][1], *split(slope), 1, dot)
-        slope = jnp.concatenate([slope, slope], axis=0)
+        slopes.append(jnp.concatenate([slope, slope], axis=0))
+    for corner, slope in enumerate(slopes):
         ge = jnp.concatenate(
             [e_ref[corner, :, s * grid : (s + 1) * grid] * slope for s in range(local_src)], axis=1
         )

time: 23.7 us -> 23.3 us (0.983)
  Pallas kernels: 21.9 us -> 21.6 us
    pallas_call x1, Pallas kernels: 21.9 us -> 21.6 us  [per_device(): pl.pallas_call(functools.partial(kernel, (ns, nf, nt, local_src, corners,...]
where the time goes in v7:
time: 23.3 us; the launch traced here: 23.2 us
  Pallas kernels  21.6 us (93%)
  local copies, waits for them, and re-layouts  1.58 us (7%)
    pallas_call x1, Pallas kernels, per_device(): pl.pallas_call(functools.partial(kernel, (ns, nf, nt, local_src, corners,...  21.6 us
    unnamed x1, local copies, waits for them, and re-layouts  1.58 us

profile of v7, /device:TPU:0, one launch (start us, length us, event | category | flops | bytes accessed | tf_op | source)
XLA Modules:
  0.0 23.2 jit_solution(7411160622161842627)
XLA Ops:
  0.0 21.6 %abbe_gradient.1 = f32[96,384]{1,0:T(8,128)} custom-call(s32[4]{0:T(128)} %counts_ref.1, f32[8]{0:T(128)} %w_ref.1, f32[384,384]{1,0:T(8,128)} %mask_hbm.1, f32[384,384]{1,0:T(8,128)} %target_hbm.1, f32[2,8,2,64,64]{4,3,2,1,0:T(8,128)} %pup_hbm.1, bf16[2,128,384]{2,1,0:T(8,128)(2,1)} %constant.16.clone.refs_0_.refs_3_, ...), custom_call_target="tpu_custom_call" | custom-call | tf_op jit(solution)/shard_map/abbe_gradient/pallas_call | solution.py:400
  21.6 1.6 %copy.16 = f32[96,384]{1,0:T(8,128)} copy(f32[96,384]{1,0:T(8,128)} %abbe_gradient.1) | data formatting | bytes 294912

commit v8 on v7

--- a/solution.py
+++ b/solution.py
@@ -28,7 +28,9 @@
     win = tile + 2 * width
     grid = 2 * freqs
     k = np.arange(freqs) - freqs // 2
-    row = 2.0 * np.pi * ((k[:, None] * (np.arange(tile) + width)[None, :]) % win) / win
+    even, odd = np.flatnonzero(k % 2 == 0), np.flatnonzero(k % 2)
+    order = np.concatenate([even, odd])
+    row = 2.0 * np.pi * ((k[order][:, None] * (np.arange(tile) + width)[None, :]) % win) / win
     row2 = np.concatenate([np.cos(row), -np.sin(row)], axis=0) / math.sqrt(win)
     col = 2.0 * np.pi * ((k[:, None] * np.arange(win)[None, :]) % win) / win
     col2 = np.concatenate([np.cos(col), -np.sin(col)], axis=0) / math.sqrt(win)
@@ -39,6 +41,12 @@
     at = 2.0 * np.pi * ((k[:, None] * np.arange(grid)[None, :]) % grid) / grid
     c, s = np.cos(at) * math.sqrt(2.0 / freqs), np.sin(at) * math.sqrt(2.0 / freqs)
     field = np.block([[c, s], [-s, c]])
+
+    def by_parity(chosen):
+        points = np.concatenate([np.arange(freqs), grid + np.arange(freqs)])
+        high, low = halves(field.T[points][:, np.concatenate([chosen, freqs + chosen])])
+        return np.concatenate([high, low, high, low], axis=1)
+
     q = np.arange(1 - freqs, freqs)
     gap = (np.arange(tile) + width)[:, None] / win - np.arange(grid)[None, :] / grid
     fine = np.cos(2.0 * np.pi * gap[:, :, None] * q[None, None, :]).sum(-1) / grid
@@ -48,7 +56,8 @@
         left=halves(edges[0]),
         right=halves(edges[1]),
         f1=halves(field),
-        f2=halves(field.T),
+        f2=np.stack([by_parity(even), by_parity(odd)]),
+        f3=halves(field[np.concatenate([order, freqs + order])]),
         fine=halves(fine),
         finet=halves(fine.T),
         rowt=halves(row2.T),
@@ -99,7 +108,7 @@
     return both[:, :size] + (both[:, size:] + product(low, table_high))
 
 
-NAMES = ("row", "left", "right", "own", "f1", "f2", "fine", "finet", "rowt")
+NAMES = ("row", "left", "right", "own", "f1", "f2", "f3", "fine", "finet", "rowt")
 
 
 def kernel(dims, counts_ref, w_ref, mask_hbm, target_hbm, pup_hbm, *refs):
@@ -183,7 +192,7 @@
     need("row", "mask", "left", "right")
     load("own", held["own"], tab["own"])
     load("pupil", pup_hbm, pup_ref)
-    for name in ("f1", "f2", "fine"):
+    for name in ("f1", "f2", "f3", "fine"):
         load(name, held[name], tab[name])
     load("target", target_hbm, target_ref)
     load("finet", held["finet"], tab["finet"])
@@ -208,6 +217,7 @@
     pl.when(has_left)(zs_left.start)
     pl.when(has_right)(zs_right.start)
     mh, ml = split(table_times(tab["row"], mask_ref[:, edge : tile - edge]))
+    few = freqs // 2
     need("own")
     spec = columns(
         jnp.concatenate([sh[:, :edge], mh, sh[:, edge:]], axis=1),
@@ -218,7 +228,14 @@
     for corner in range(corners):
         for s in range(local_src):
             p_ref[corner, s] = jnp.concatenate(
-                [pup_ref[0, s, corner], pup_ref[1, s, corner]], axis=1
+                [
+                    jnp.concatenate(
+                        [pup_ref[n, s, corner, pl.ds(m, few, stride=2), :] for m in range(2)],
+                        axis=0,
+                    )
+                    for n in range(2)
+                ],
+                axis=1,
             )
     pl.when(has_left)(zs_right.wait_recv)
     pl.when(has_right)(zs_left.wait_recv)
@@ -235,17 +252,32 @@
             p = p_ref[corner, s]
             parts.append(p * same + swap(p) * cross)
         h = times_table(jnp.concatenate(parts, axis=0), tab["f1"])
-        h = jnp.concatenate(
-            [
-                jnp.concatenate(
-                    [h[s * freqs : (s + 1) * freqs, :grid], h[s * freqs : (s + 1) * freqs, grid:]],
-                    axis=0,
+        h_high, h_low = split(h)
+
+        def parity(n):
+            def pieces(x):
+                return jnp.concatenate(
+                    [
+                        jnp.concatenate(
+                            [
+                                x[s * freqs + n * few : s * freqs + (n + 1) * few, :grid],
+                                x[s * freqs + n * few : s * freqs + (n + 1) * few, grid:],
+                            ],
+                            axis=0,
+                        )
+                        for s in range(local_src)
+                    ],
+                    axis=1,
                 )
-                for s in range(local_src)
-            ],
-            axis=1,
-        )
-        e = table_times(tab["f2"], h)
+
+            high, low = pieces(h_high), pieces(h_low)
+            return dot(tab["f2"][n], jnp.concatenate([high, high, low, low], axis=0))
+
+        h_even, h_odd = parity(0), parity(1)
+        plus, minus = h_even + h_odd, h_even - h_odd
+        e = jnp.concatenate(
+            [plus[:freqs], minus[:freqs], plus[freqs:], minus[freqs:]], axis=0
+        )
         e_ref[corner] = e
         total = jnp.zeros((grid, grid), jnp.float32)
         for s in range(local_src):
@@ -261,7 +293,7 @@
             copy.start()
             i_copies.append(copy)
 
-    need("fine", "target", "finet", "rowt")
+    need("f3", "fine", "target", "finet", "rowt")
     count = counts_ref[t]
     sum_x = jnp.zeros((freqs, grid), jnp.float32)
     sum_y = jnp.zeros((freqs, grid), jnp.float32)
@@ -282,7 +314,7 @@
         ge = jnp.concatenate(
             [e_ref[corner, :, s * grid : (s + 1) * grid] * slope for s in range(local_src)], axis=1
         )
-        gh = table_times(tab["f1"], ge)
+        gh = table_times(tab["f3"], ge)
         gh = jnp.concatenate(
             [
                 jnp.concatenate(

time: 23.3 us -> 23.1 us (level)
  no operation moved by 1% of the time
where the time goes in v8:
time: 23.1 us; the launch traced here: 23 us
  Pallas kernels  21.4 us (93%)
  local copies, waits for them, and re-layouts  1.58 us (7%)
    pallas_call x1, Pallas kernels, per_device(): pl.pallas_call(functools.partial(kernel, (ns, nf, nt, local_src, corners,...  21.4 us
    unnamed x1, local copies, waits for them, and re-layouts  1.58 us

profile of v8, /device:TPU:0, one launch (start us, length us, event | category | flops | bytes accessed | tf_op | source)
XLA Modules:
  0.0 23.0 jit_solution(535251308528819701)
XLA Ops:
  0.0 21.4 %abbe_gradient.1 = f32[96,384]{1,0:T(8,128)} custom-call(s32[4]{0:T(128)} %counts_ref.1, f32[8]{0:T(128)} %w_ref.1, f32[384,384]{1,0:T(8,128)} %mask_hbm.1, f32[384,384]{1,0:T(8,128)} %target_hbm.1, f32[2,8,2,64,64]{4,3,2,1,0:T(8,128)} %pup_hbm.1, bf16[2,128,384]{2,1,0:T(8,128)(2,1)} %constant.20.clone.refs_0_, bf16[2,128,128]{2,1,0:T(8,128)(2,1)} %constant.21.clone.refs_1_, ...), custom_call_target="tpu_custom_call" | custom-call | tf_op jit(solution)/shard_map/abbe_gradient/pallas_call | solution.py:432
  21.4 1.6 %copy.17 = f32[96,384]{1,0:T(8,128)} copy(f32[96,384]{1,0:T(8,128)} %abbe_gradient.1) | data formatting | bytes 294912

commit v9 on v8

--- a/solution.py
+++ b/solution.py
@@ -303,12 +303,12 @@
         for a in range(1, ns):
             i_copies[corner * (ns - 1) + a - 1].wait_recv()
             total = total + i_recv[a - 1, corner]
-        intensity = times_turned(table_times(tab["fine"], total), tab["fine"])
+        intensity = table_times(tab["fine"], times_turned(total, tab["fine"]))
         wave = jnp.tanh((0.5 * resist_slope) * (intensity - resist_level))
         active = jnp.where(focus * corners + corner < count, 0.25 * resist_slope, 0.0)
         slope = active * ((1.0 - 2.0 * target_ref[...]) + wave) * (1.0 - wave * wave)
+        slope = table_times(tab["finet"], slope)
         slope = narrow(*split(slope), tab["fine"][0], tab["fine"][1], 1, dot)
-        slope = narrow(tab["finet"][0], tab["finet"][1], *split(slope), 1, dot)
         slopes.append(jnp.concatenate([slope, slope], axis=0))
     for corner, slope in enumerate(slopes):
         ge = jnp.concatenate(

time: 23.1 us -> 23.4 us (1.013)
  Pallas kernels: 21.4 us -> 21.7 us
    pallas_call x1, Pallas kernels: 21.4 us -> 21.7 us  [per_device(): pl.pallas_call(functools.partial(kernel, (ns, nf, nt, local_src, corners,...]
where the time goes in v9:
time: 23.4 us; the launch traced here: 23.3 us
  Pallas kernels  21.7 us (93%)
  local copies, waits for them, and re-layouts  1.58 us (7%)
    pallas_call x1, Pallas kernels, per_device(): pl.pallas_call(functools.partial(kernel, (ns, nf, nt, local_src, corners,...  21.7 us
    unnamed x1, local copies, waits for them, and re-layouts  1.58 us

profile of v9, /device:TPU:0, one launch (start us, length us, event | category | flops | bytes accessed | tf_op | source)
XLA Modules:
  0.0 23.3 jit_solution(4712056774372096569)
XLA Ops:
  0.0 21.7 %abbe_gradient.1 = f32[96,384]{1,0:T(8,128)} custom-call(s32[4]{0:T(128)} %counts_ref.1, f32[8]{0:T(128)} %w_ref.1, f32[384,384]{1,0:T(8,128)} %mask_hbm.1, f32[384,384]{1,0:T(8,128)} %target_hbm.1, f32[2,8,2,64,64]{4,3,2,1,0:T(8,128)} %pup_hbm.1, bf16[2,128,384]{2,1,0:T(8,128)(2,1)} %constant.20.clone.refs_0_, bf16[2,128,128]{2,1,0:T(8,128)(2,1)} %constant.21.clone.refs_1_, ...), custom_call_target="tpu_custom_call" | custom-call | tf_op jit(solution)/shard_map/abbe_gradient/pallas_call | solution.py:432
  21.7 1.6 %copy.17 = f32[96,384]{1,0:T(8,128)} copy(f32[96,384]{1,0:T(8,128)} %abbe_gradient.1) | data formatting | bytes 294912

commit v10 on v8

--- a/solution.py
+++ b/solution.py
@@ -413,6 +413,17 @@
         copy.wait_send()
 
 
+def handed_on(step, source, dest, sems):
+    copies = []
+    for n, begin in enumerate(range(0, source.shape[0], step)):
+        rows = pl.ds(begin, step)
+        copies.append(pltpu.make_async_copy(source.at[rows, :], dest.at[rows, :], sems.at[n]))
+    for copy in copies:
+        copy.start()
+    for copy in copies:
+        copy.wait()
+
+
 def per_device(mask, target, pupil, weights, counts):
     tile = mask.shape[0]
     freqs = pupil.shape[-1]
@@ -429,7 +440,7 @@
     hbm = pl.BlockSpec(memory_space=pltpu.HBM)
     f32 = jnp.float32
     dma = pltpu.SemaphoreType.DMA
-    return pl.pallas_call(
+    result = pl.pallas_call(
         functools.partial(kernel, (ns, nf, nt, local_src, corners, freqs, tile)),
         out_shape=jax.ShapeDtypeStruct((rows, tile), f32),
         in_specs=[smem, smem] + [hbm] * (3 + len(NAMES)),
@@ -470,6 +481,16 @@
         ),
         name="abbe_gradient",
     )(counts, weights, mask, target, pupil, *[held[name] for name in NAMES])
+    step = 8 * max(1, rows // 32)
+    return pl.pallas_call(
+        functools.partial(handed_on, step),
+        out_shape=jax.ShapeDtypeStruct((rows, tile), f32),
+        in_specs=[hbm],
+        out_specs=hbm,
+        scratch_shapes=[dma((rows // step,))],
+        compiler_params=pltpu.CompilerParams(vmem_limit_bytes=64 * 1024 * 1024),
+        name="hand_on",
+    )(result)
 
 
 def solution(mesh):

time: 23.1 us -> 27.2 us (1.18)
  Pallas kernels: 21.4 us -> 27 us
  local copies, waits for them, and re-layouts: 1.58 us -> 0 us
    pallas_call x0 -> x1, Pallas kernels: none -> 5.61 us  [per_device(): pl.pallas_call(functools.partial(handed_on, step), out_shape=jax.ShapeDty...]
    unnamed x1 -> x0, local copies, waits for them, and re-layouts: 1.58 us -> none
where the time goes in v10:
time: 27.2 us; the launch traced here: 27 us
  Pallas kernels  27 us (99%)
    pallas_call x1, Pallas kernels, per_device(): pl.pallas_call(functools.partial(kernel, (ns, nf, nt, local_src, corners,...  21.4 us
    pallas_call x1, Pallas kernels, per_device(): pl.pallas_call(functools.partial(handed_on, step), out_shape=jax.ShapeDty...  5.61 us

profile of v10, /device:TPU:0, one launch (start us, length us, event | category | flops | bytes accessed | tf_op | source)
XLA Modules:
  0.0 27.0 jit_solution(2737654312462032431)
XLA Ops:
  0.0 21.4 %abbe_gradient.1.source = f32[96,384]{1,0:T(8,128)} custom-call(s32[4]{0:T(128)} %counts_ref.1, f32[8]{0:T(128)} %w_ref.1, f32[384,384]{1,0:T(8,128)} %mask_hbm.1, f32[384,384]{1,0:T(8,128)} %target_hbm.1, f32[2,8,2,64,64]{4,3,2,1,0:T(8,128)} %pup_hbm.1, bf16[2,128,384]{2,1,0:T(8,128)(2,1)} %constant.20.clone.refs_0_, ...), custom_call_target="tpu_custom_call" | custom-call | tf_op jit(solution)/shard_map/abbe_gradient/pallas_call | solution.py:443
  21.4 5.6 %hand_on.1 = f32[96,384]{1,0:T(8,128)} custom-call(f32[96,384]{1,0:T(8,128)} %abbe_gradient.1.source), custom_call_target="tpu_custom_call" | custom-call | tf_op jit(solution)/shard_map/hand_on/pallas_call | solution.py:485

commit v11 on v8

--- a/solution.py
+++ b/solution.py
@@ -152,9 +152,15 @@
         loads[name].start()
 
     load("row", held["row"], tab["row"])
-    load("mask", mask_hbm, mask_ref)
-    for name in ("left", "right"):
-        load(name, held[name], tab[name])
+    edge = 2 * AMBIT
+    for name, at, size in (
+        ("first", 0, edge), ("last", tile - edge, edge), ("middle", edge, tile - 2 * edge)
+    ):
+        if name == "middle":
+            for side in ("left", "right"):
+                load(side, held[side], tab[side])
+        place = pl.ds(at, size)
+        load(name, mask_hbm.at[:, place], mask_ref.at[:, place])
 
     def need(*names):
         for name in names:
@@ -189,7 +195,7 @@
         top, low = q[:freqs], swap(q[freqs:])
         return jnp.where(first, top - low, top + low)
 
-    need("row", "mask", "left", "right")
+    need("row", "first", "last")
     load("own", held["own"], tab["own"])
     load("pupil", pup_hbm, pup_ref)
     for name in ("f1", "f2", "f3", "fine"):
@@ -198,14 +204,13 @@
     load("finet", held["finet"], tab["finet"])
     load("rowt", held["rowt"].at[:, pl.ds(begin, rows), :], tab["rowt"])
 
-    edge = 2 * AMBIT
-
     def columns(high, low, table):
         wide = jnp.concatenate([table[0], table[1], table[0]], axis=1)
         return complex_of(dot_t(jnp.concatenate([high, high, low], axis=1), wide))
 
     sides = jnp.concatenate([mask_ref[:, :edge], mask_ref[:, tile - edge :]], axis=1)
     sh, sl = split(table_times(tab["row"], sides))
+    need("left", "right")
     zs_send[0] = columns(sh[:, :edge], sl[:, :edge], tab["left"])
     zs_send[1] = columns(sh[:, edge:], sl[:, edge:], tab["right"])
     pl.semaphore_wait(
@@ -216,6 +221,7 @@
     zs_right = remote(zs_send.at[1], zs_recv.at[0], zs_ss.at[1], zs_rs.at[0], {"tile": right})
     pl.when(has_left)(zs_left.start)
     pl.when(has_right)(zs_right.start)
+    need("middle")
     mh, ml = split(table_times(tab["row"], mask_ref[:, edge : tile - edge]))
     few = freqs // 2
     need("own")
@@ -442,7 +448,7 @@
                 pltpu.VMEM((2, rows, grid) if name == "rowt" else held[name].shape, jnp.bfloat16)
                 for name in NAMES
             ],
-            dma((len(NAMES) + 3,)),
+            dma((len(NAMES) + 5,)),
             pltpu.VMEM((corners, local_src, freqs, grid), f32),
             pltpu.VMEM((corners, 2 * grid, local_src * grid), f32),
             pltpu.VMEM((2, freqs, grid), f32),

time: 23.1 us -> 23.2 us (level)
  no operation moved by 1% of the time
where the time goes in v11:
time: 23.2 us; the launch traced here: 23 us
  Pallas kernels  21.4 us (92%)
  local copies, waits for them, and re-layouts  1.58 us (7%)
    pallas_call x1, Pallas kernels, per_device(): pl.pallas_call(functools.partial(kernel, (ns, nf, nt, local_src, corners,...  21.4 us
    unnamed x1, local copies, waits for them, and re-layouts  1.58 us

profile of v11, /device:TPU:0, one launch (start us, length us, event | category | flops | bytes accessed | tf_op | source)
XLA Modules:
  0.0 23.0 jit_solution(17352482091209439729)
XLA Ops:
  0.0 21.4 %abbe_gradient.1 = f32[96,384]{1,0:T(8,128)} custom-call(s32[4]{0:T(128)} %counts_ref.1, f32[8]{0:T(128)} %w_ref.1, f32[384,384]{1,0:T(8,128)} %mask_hbm.1, f32[384,384]{1,0:T(8,128)} %target_hbm.1, f32[2,8,2,64,64]{4,3,2,1,0:T(8,128)} %pup_hbm.1, bf16[2,128,384]{2,1,0:T(8,128)(2,1)} %constant.20.clone.refs_0_, bf16[2,128,128]{2,1,0:T(8,128)(2,1)} %constant.21.clone.refs_1_, ...), custom_call_target="tpu_custom_call" | custom-call | tf_op jit(solution)/shard_map/abbe_gradient/pallas_call | solution.py:438
  21.4 1.6 %copy.17 = f32[96,384]{1,0:T(8,128)} copy(f32[96,384]{1,0:T(8,128)} %abbe_gradient.1) | data formatting | bytes 294912

commit v12 on v8

--- a/solution.py
+++ b/solution.py
@@ -155,6 +155,7 @@
     load("mask", mask_hbm, mask_ref)
     for name in ("left", "right"):
         load(name, held[name], tab[name])
+    load("pupil", pup_hbm, pup_ref)
 
     def need(*names):
         for name in names:
@@ -191,7 +192,6 @@
 
     need("row", "mask", "left", "right")
     load("own", held["own"], tab["own"])
-    load("pupil", pup_hbm, pup_ref)
     for name in ("f1", "f2", "f3", "fine"):
         load(name, held[name], tab[name])
     load("target", target_hbm, target_ref)

time: 23.1 us -> 23.1 us (level)
  no operation moved by 1% of the time
where the time goes in v12:
time: 23.1 us; the launch traced here: 23 us
  Pallas kernels  21.4 us (93%)
  local copies, waits for them, and re-layouts  1.58 us (7%)
    pallas_call x1, Pallas kernels, per_device(): pl.pallas_call(functools.partial(kernel, (ns, nf, nt, local_src, corners,...  21.4 us
    unnamed x1, local copies, waits for them, and re-layouts  1.58 us

profile of v12, /device:TPU:0, one launch (start us, length us, event | category | flops | bytes accessed | tf_op | source)
XLA Modules:
  0.0 23.0 jit_solution(7564140730640511713)
XLA Ops:
  0.0 21.4 %abbe_gradient.1 = f32[96,384]{1,0:T(8,128)} custom-call(s32[4]{0:T(128)} %counts_ref.1, f32[8]{0:T(128)} %w_ref.1, f32[384,384]{1,0:T(8,128)} %mask_hbm.1, f32[384,384]{1,0:T(8,128)} %target_hbm.1, f32[2,8,2,64,64]{4,3,2,1,0:T(8,128)} %pup_hbm.1, bf16[2,128,384]{2,1,0:T(8,128)(2,1)} %constant.20.clone.refs_0_, bf16[2,128,128]{2,1,0:T(8,128)(2,1)} %constant.21.clone.refs_1_, ...), custom_call_target="tpu_custom_call" | custom-call | tf_op jit(solution)/shard_map/abbe_gradient/pallas_call | solution.py:432
  21.4 1.6 %copy.17 = f32[96,384]{1,0:T(8,128)} copy(f32[96,384]{1,0:T(8,128)} %abbe_gradient.1) | data formatting | bytes 294912
